TPU v7x, 128 devices: a whole 4x4x4 slice. The times are simulated.
128 devices in a mesh: dp: 8 (over x, core), ctx: 16 (over z, y).
Axes of the slice: x: 4, y: 4, z: 4, core: 2. Of those that a mesh axis runs over, the one named last changes fastest.
Arguments:
- queries: bfloat16 [8, 2048, 4096], P('dp', 'ctx'), may hold values from -6 to 6
- key_inputs: bfloat16 [8, 2048, 4096], P('dp', 'ctx'), may hold values from -6 to 6
- value_inputs: bfloat16 [8, 2048, 4096], P('dp', 'ctx'), may hold values from -6 to 6
- cotangent: bfloat16 [8, 2048, 4096], P('dp', 'ctx'), may hold values from -3 to 3
- filter_taps: float32 [1024, 4096], P(None, 'ctx')
- skip_gain: float32 [4096], P('ctx'), may hold values from -4 to 4
- lengths: int32 [8, 3], P('dp'), may hold values from 1 to 1024, 2048 in all within a row
Outputs:
- mixed_out: bfloat16 [8, 2048, 4096], P('dp', 'ctx')
- query_grad: bfloat16 [8, 2048, 4096], P('dp', 'ctx')
- key_grad: bfloat16 [8, 2048, 4096], P('dp', 'ctx')
- value_grad: bfloat16 [8, 2048, 4096], P('dp', 'ctx')
- filter_grad: float32 [1024, 4096], P('dp', 'ctx')
Inputs may be any that keep to these rules, and one draw needn't show every extreme that they name: Each row holds the lengths of 3 windows that fill the slice of 2048 positions in order; they sum to 2048 and the largest is exactly half of 2048.
All inputs are finite; a program needn't handle non-finite values.
Results may differ from a plain program's by a relative error of at most 0.017.
Values may be sent and summed in bfloat16 or wider, within the bound.
No kernel may reach another device: no remote copies, remote signals or barrier semaphores. Data moves between devices by JAX's collectives and lax.ppermute only.
A program may use at most 192 MiB of HBM per device.

v0:
```python
import math

import jax
import jax.numpy as jnp
from jax import lax
from jax.sharding import PartitionSpec as P


def window_masks(length_row, total):
    starts = jnp.cumsum(length_row) - length_row
    places = jnp.arange(total, dtype=jnp.int32)
    inside = (places[None, :] >= starts[:, None]) & (
        places[None, :] < (starts + length_row)[:, None]
    )
    return inside.astype(jnp.float32)[:, :, None]


def dft_tables(padded):
    outer = 64
    inner = padded // outer
    k_outer = jnp.arange(outer, dtype=jnp.int32)
    n_inner = jnp.arange(inner, dtype=jnp.int32)
    angle_one = (k_outer[:, None] * k_outer[None, :] % outer).astype(jnp.float32) * (
        -2.0 * math.pi / outer
    )
    cos_one = jnp.cos(angle_one)
    sin_one = jnp.sin(angle_one)
    first = jnp.stack([cos_one, sin_one], 0)
    back_first = jnp.stack([cos_one, sin_one], 1)
    twist = (k_outer[:, None] * n_inner[None, :] % padded).astype(jnp.float32) * (
        -2.0 * math.pi / padded
    )
    twist_re = jnp.cos(twist)[:, :, None]
    twist_im = jnp.sin(twist)[:, :, None]
    back_re = jnp.cos(twist).T[:, :, None]
    back_im = jnp.sin(twist).T[:, :, None]
    angle_two = (n_inner[:, None] * n_inner[None, :] % inner).astype(jnp.float32) * (
        -2.0 * math.pi / inner
    )
    cos_two = jnp.cos(angle_two)
    sin_two = jnp.sin(angle_two)
    second = jnp.stack([jnp.stack([cos_two, sin_two], 1), jnp.stack([-sin_two, cos_two], 1)], 0)
    return (first, twist_re, twist_im, second, back_first, back_re, back_im)


def forward_dft(field, tables):
    first, twist_re, twist_im, second, back_first, back_re, back_im = tables
    outer = first.shape[1]
    inner = second.shape[1]
    shaped = field.reshape(outer, inner, field.shape[1])
    section = jnp.einsum("rka,abc->rkbc", first, shaped, precision=lax.Precision.HIGHEST)
    turned = jnp.stack(
        [
            section[0] * twist_re - section[1] * twist_im,
            section[0] * twist_im + section[1] * twist_re,
        ],
        0,
    )
    return jnp.einsum("rkbc,rbql->qlkc", turned, second, precision=lax.Precision.HIGHEST)


def inverse_dft(spectral, tables):
    first, twist_re, twist_im, second, back_first, back_re, back_im = tables
    outer = first.shape[1]
    inner = second.shape[1]
    section = jnp.einsum("qbrl,rlkc->qbkc", second, spectral, precision=lax.Precision.HIGHEST)
    turned = jnp.stack(
        [section[0] * back_re + section[1] * back_im, section[1] * back_re - section[0] * back_im],
        0,
    )
    result = jnp.einsum("aqk,qbkc->abc", back_first, turned, precision=lax.Precision.HIGHEST)
    return result.reshape(outer * inner, spectral.shape[3]) / (1.0 * outer * inner)


def times_spec(left, right):
    return jnp.stack(
        [left[0] * right[0] - left[1] * right[1], left[0] * right[1] + left[1] * right[0]], 0
    )


def times_conj(left, right):
    return jnp.stack(
        [left[0] * right[0] + left[1] * right[1], left[1] * right[0] - left[0] * right[1]], 0
    )


def forward_mix(product_cols, taps, skip_gain, masks, tables):
    product_wide = lax.optimization_barrier(product_cols).astype(jnp.float32)
    convolved = jnp.zeros(product_wide.shape, jnp.float32)
    saved = []
    for index in range(masks.shape[0]):
        part = forward_dft(masks[index] * product_wide, tables)
        saved.append(part)
        convolved = convolved + masks[index] * inverse_dft(times_spec(taps, part), tables)
    mixing = (convolved + skip_gain[None, :] * product_wide).astype(jnp.bfloat16)
    return (mixing, saved)


def backward_mix(delta_cols, taps, skip_gain, masks, tables, saved):
    delta_wide = lax.optimization_barrier(delta_cols).astype(jnp.float32)
    back = jnp.zeros(delta_wide.shape, jnp.float32)
    cross = None
    for index in range(masks.shape[0]):
        grad_spec = forward_dft(masks[index] * delta_wide, tables)
        back = back + masks[index] * inverse_dft(times_conj(grad_spec, taps), tables)
        term = times_conj(grad_spec, saved[index])
        cross = term if cross is None else cross + term
    units = (back + skip_gain[None, :] * delta_wide).astype(jnp.bfloat16)
    return (units, inverse_dft(cross, tables))


def shards(queries, key_inputs, value_inputs, cotangent, filter_taps, skip_gain, lengths):
    reach = filter_taps.shape[0]
    span = 2 * reach
    tables = dft_tables(span)
    masks = window_masks(lengths[0], span)
    taps = forward_dft(jnp.pad(filter_taps, ((0, reach), (0, 0))), tables)
    key_wide = key_inputs.astype(jnp.float32)
    value_wide = value_inputs.astype(jnp.float32)
    product = (key_wide * value_wide).astype(jnp.bfloat16)
    product_cols = lax.all_to_all(product, "ctx", split_axis=2, concat_axis=1, tiled=True)
    mixing, saved = forward_mix(product_cols[0], taps, skip_gain, masks, tables)
    mixing_rows = lax.all_to_all(mixing[None], "ctx", split_axis=1, concat_axis=2, tiled=True)
    mixing_wide = lax.optimization_barrier(mixing_rows).astype(jnp.float32)
    query_wide = queries.astype(jnp.float32)
    cot_wide = cotangent.astype(jnp.float32)
    mixed_out = (query_wide * mixing_wide).astype(jnp.bfloat16)
    query_grad = (cot_wide * mixing_wide).astype(jnp.bfloat16)
    delta = (cot_wide * query_wide).astype(jnp.bfloat16)
    delta_cols = lax.all_to_all(delta, "ctx", split_axis=2, concat_axis=1, tiled=True)
    units, filter_local = backward_mix(delta_cols[0], taps, skip_gain, masks, tables, saved)
    units_rows = lax.all_to_all(units[None], "ctx", split_axis=1, concat_axis=2, tiled=True)
    units_wide = lax.optimization_barrier(units_rows).astype(jnp.float32)
    key_grad = (units_wide * value_wide).astype(jnp.bfloat16)
    value_grad = (units_wide * key_wide).astype(jnp.bfloat16)
    filter_grad = lax.psum_scatter(
        filter_local[:reach].astype(jnp.bfloat16), "dp", scatter_dimension=0, tiled=True
    ).astype(jnp.float32) / lax.axis_size("dp")
    return (mixed_out, query_grad, key_grad, value_grad, filter_grad)


def solution(mesh):
    in_specs = (
        P("dp", "ctx", None),
        P("dp", "ctx", None),
        P("dp", "ctx", None),
        P("dp", "ctx", None),
        P(None, "ctx"),
        P("ctx"),
        P("dp", None),
    )
    out_specs = (
        P("dp", "ctx", None),
        P("dp", "ctx", None),
        P("dp", "ctx", None),
        P("dp", "ctx", None),
        P("dp", "ctx"),
    )
    return jax.shard_map(shards, mesh=mesh, in_specs=in_specs, out_specs=out_specs, check_vma=False)
```

profile of v0, /device:TPU:0, one launch (start us, length us, event | category | flops | bytes accessed | tf_op | source)
XLA Modules:
  0.0 498.2 jit_solution(4505039444336725196)
XLA Ops:
  9.9 17.0 %copy.405 = bf16[1,128,4096]{1,0,2:T(2,128)(2,1)} copy(bf16[1,128,4096]{1,2,0:T(8,128)(2,1)S(1)} %fusion.102) | data formatting | bytes 2097152 | tf_op jit(solution)/shard_map/convert_element_type | solution.py:129
  27.4 23.4 %reduce = bf16[4096,128]{1,0:T(8,128)(2,1)S(1)} reduce(bf16[4096,1,128]{2,1,0:T(2,128)(2,1)} %bitcast.315, bf16[]{:T(256)} %broadcast.500), dimensions={1}, to_apply=%bitcast.298.reduce_sub_computation | reduce | bytes 2097154
  52.0 8.5 %all-to-all-start.2 = ((bf16[16,2,16384]{2,1,0:T(2,128)(2,1)}), bf16[16,2,16384]{2,1,0:T(2,128)(2,1)}, u32[]{:S(2)}, u32[]{:S(2)}) async-start(bf16[16,2,16384]{2,1,0:T(2,128)(2,1)} %reshape.446), calls=%async_computation.2 | async-start | bytes 2097152 | tf_op jit(solution)/shard_map/all_to_all | solution.py:130
  61.7 5.8 %fusion.125 = f32[2,64,32,256]{3,1,2,0:T(8,128)} fusion(f32[64,32,256]{2,1,0:T(8,128)S(1)} %bitcast.305, f32[1,64,64]{2,1,0:T(8,128)S(1)} %get-tuple-element.105, f32[1,64,64]{2,1,0:T(8,128)S(1)} %get-tuple-element.106), kind=kOutput, calls=%fused_computation.138 | convolution fusion | flops 805314560 | bytes 6324224 | tf_op jit(solution)/shard_map/rka,abc->rkbc/dot_general | solution.py:51
  67.4 10.7 %all-to-all-done.2 = bf16[16,2,16384]{2,1,0:T(2,128)(2,1)} async-done(((bf16[16,2,16384]{2,1,0:T(2,128)(2,1)}), bf16[16,2,16384]{2,1,0:T(2,128)(2,1)}, u32[]{:S(2)}, u32[]{:S(2)}) %all-to-all-start.2) | async-done | bytes 1048608 | tf_op jit(solution)/shard_map/all_to_all | solution.py:130
  95.4 14.8 %fusion.115 = f32[2,64,32,256]{3,1,2,0:T(8,128)S(1)} fusion(f32[64,32,256]{2,1,0:T(8,128)S(1)} %bitcast.313, f32[1,64,64]{2,1,0:T(8,128)S(1)} %get-tuple-element.105, f32[1,64,64]{2,1,0:T(8,128)S(1)} %get-tuple-element.106), kind=kOutput, calls=%fused_computation.125 | convolution fusion | flops 805314560 | bytes 6324224 | tf_op jit(solution)/shard_map/rka,abc->rkbc/dot_general | solution.py:51
  110.2 6.2 %multiply_subtract_fusion.12 = (f32[1,64,32,256]{3,1,2,0:T(8,128)S(1)}, f32[1,64,32,256]{3,1,2,0:T(8,128)}, f32[1,64,32,256]{3,1,2,0:T(8,128)}, f32[1,64,32,256]...) fusion(f32[2,64,32,256]{3,1,2,0:T(8,128)S(1)} %fusion.115, ...), kind=kLoop, calls=%fused_computation.172 | loop fusion | flops 12582912 | bytes 33570816 | tf_op jit(solution)/shard_map/sub | solution.py:54
  120.4 6.2 %fusion.90 = f32[2,32,64,256]{3,1,2,0:T(8,128)S(1)} fusion(f32[2,64,32,256]{3,1,2,0:T(8,128)S(1)} %pad_maximum_fusion.16, f32[1,32,2,32]{1,3,0,2:T(8,128)S(1)} %get-tuple-element.104, f32[1,32,2,32]{1,3,0,2:T(8,128)S(1)} %get-tuple-element.103), kind=kOutput, calls=%fused_computation.103 | convolution fusion | flops 805310464 | bytes 8404992 | tf_op jit(solution)/shard_map/rkbc,rbql->qlkc/dot_general | solution.py:59
  126.7 6.4 %fusion.57 = f32[2,32,64,256]{3,1,2,0:T(8,128)S(1)} fusion(f32[2,64,32,256]{3,1,2,0:T(8,128)S(1)} %pad_maximum_fusion, f32[1,32,2,32]{1,3,0,2:T(8,128)S(1)} %get-tuple-element.104, f32[1,32,2,32]{1,3,0,2:T(8,128)S(1)} %get-tuple-element.103), kind=kOutput, calls=%fused_computation.92 | convolution fusion | flops 805310464 | bytes 8404992 | tf_op jit(solution)/shard_map/rkbc,rbql->qlkc/dot_general | solution.py:59
  133.6 6.0 %fusion.84 = f32[2,32,64,256]{3,1,2,0:T(8,128)S(1)} fusion(f32[2,64,32,256]{3,1,2,0:T(8,128)S(1)} %pad_maximum_fusion.13, f32[1,32,2,32]{1,3,0,2:T(8,128)S(1)} %get-tuple-element.104, f32[1,32,2,32]{1,3,0,2:T(8,128)S(1)} %get-tuple-element.103), kind=kOutput, calls=%fused_computation.101 | convolution fusion | flops 805310464 | bytes 8404992 | tf_op jit(solution)/shard_map/rkbc,rbql->qlkc/dot_general | solution.py:59
  140.0 6.2 %fusion.78 = f32[2,32,64,256]{3,1,2,0:T(8,128)S(1)} fusion(f32[2,64,32,256]{3,1,2,0:T(8,128)S(1)} %pad_maximum_fusion.10, f32[1,32,2,32]{1,3,0,2:T(8,128)S(1)} %get-tuple-element.104, f32[1,32,2,32]{1,3,0,2:T(8,128)S(1)} %get-tuple-element.103), kind=kOutput, calls=%fused_computation.99 | convolution fusion | flops 805310464 | bytes 8404992 | tf_op jit(solution)/shard_map/rkbc,rbql->qlkc/dot_general | solution.py:59
  147.2 5.2 %fusion.93 = f32[2,32,64,256]{3,1,2,0:T(8,128)} fusion(f32[1,32,64,256]{3,1,2,0:T(8,128)S(1)} %get-tuple-element.26, f32[1,32,64,256]{3,1,2,0:T(8,128)S(1)} %get-tuple-element.25, f32[1,32,2,32]{1,3,0,2:T(8,128)S(1)} %get-tuple-element.104, f32[1,32,2,32]{1,3,0,2:T(8,128)S(1)} %get-tuple-element.103), kind=kOutput, calls=%fused_computation.104 | convolution fusion | flops 806359040 | bytes 8404992 | tf_op jit(solution)/shard_map/qbrl,rlkc->qbkc/dot_general | solution.py:66
  152.5 5.2 %multiply_add_fusion.11 = (f32[1,32,64,256]{3,1,2,0:T(8,128)}, f32[1,32,64,256]{3,1,2,0:T(8,128)}, f32[1,32,64,256]{3,1,2,0:T(8,128)}, f32[1,32,64,256]{3,1,2,0:T(8,128)}) fusion(f32[2,32,64,256]{3,1,2,0:T(8,128)S(1)} %fusion.78, f32[2,32,64,256]{3,1,2,0:T(8,128)S(1)} %fusion.57, f32[2,32,64,256]{3,1,2,0:T(8,128)S(1)} %fusion.84), kind=kLoop, calls=%fused_computation.170 | loop fusion | flops 6291456 | bytes 20971520 | tf_op jit(solution)/shard_map/add | solution.py:83
  157.6 5.6 %fusion.87 = f32[2,32,64,256]{3,1,2,0:T(8,128)S(1)} fusion(f32[1,32,64,256]{3,1,2,0:T(8,128)} %get-tuple-element.67, f32[1,32,64,256]{3,1,2,0:T(8,128)} %get-tuple-element.68, f32[1,32,2,32]{1,3,0,2:T(8,128)S(1)} %get-tuple-element.104, f32[1,32,2,32]{1,3,0,2:T(8,128)S(1)} %get-tuple-element.103), kind=kOutput, calls=%fused_computation.102 | convolution fusion | flops 806359040 | bytes 8404992 | tf_op jit(solution)/shard_map/qbrl,rlkc->qbkc/dot_general | solution.py:66
  190.2 11.7 %copy.404 = bf16[1,2048,256]{2,0,1:T(2,128)(2,1)S(1)} copy(bf16[1,2048,256]{2,1,0:T(8,128)(2,1)S(1)} %bitcast.321) | data formatting | bytes 2097152 | tf_op jit(solution)/shard_map/broadcast_in_dim | solution.py:132
  202.0 11.6 %reduce.1 = bf16[2048,256]{1,0:T(8,128)(2,1)} reduce(bf16[2048,1,256]{2,1,0:T(2,128)(2,1)S(1)} %bitcast.318, bf16[]{:T(256)} %broadcast.500), dimensions={1}, to_apply=%bitcast.297.reduce_sub_computation | reduce | bytes 2097154
  223.1 13.3 %all-to-all-done.3 = bf16[16,2,16384]{2,1,0:T(2,128)(2,1)} async-done(((bf16[16,2,16384]{2,1,0:T(2,128)(2,1)}), bf16[16,2,16384]{2,1,0:T(2,128)(2,1)}, u32[]{:S(2)}, u32[]{:S(2)}) %all-to-all-start.3) | async-done | bytes 1048608 | tf_op jit(solution)/shard_map/all_to_all | solution.py:132
  247.4 16.7 %copy.407 = bf16[1,128,4096]{1,0,2:T(2,128)(2,1)S(1)} copy(bf16[1,128,4096]{1,2,0:T(8,128)(2,1)S(1)} %get-tuple-element.71) | data formatting | bytes 2097152 | tf_op jit(solution)/shard_map/convert_element_type | solution.py:120
  264.0 23.4 %reduce.2 = bf16[4096,128]{1,0:T(8,128)(2,1)} reduce(bf16[4096,1,128]{2,1,0:T(2,128)(2,1)S(1)} %bitcast.319, bf16[]{:T(256)} %broadcast.500), dimensions={1}, to_apply=%bitcast.300.reduce_sub_computation | reduce | bytes 2097154
  288.7 18.0 %all_to_all.66 = bf16[16,2,16384]{2,1,0:T(2,128)(2,1)} all-to-all(bf16[16,2,16384]{2,1,0:T(2,128)(2,1)S(1)} %reshape.442), channel_id=1, replica_groups=mesh['dp'=8,'ctx'=16] {'ctx'}, dimensions={0} | all-to-all | bytes 2097152 | tf_op jit(solution)/shard_map/all_to_all | solution.py:121
  324.3 5.2 %fusion.123 = f32[2,64,32,256]{3,1,2,0:T(8,128)S(1)} fusion(f32[64,32,256]{2,1,0:T(8,128)S(1)} %bitcast.310, f32[1,64,64]{2,1,0:T(8,128)S(1)} %get-tuple-element.105, f32[1,64,64]{2,1,0:T(8,128)S(1)} %get-tuple-element.106), kind=kOutput, calls=%fused_computation.136 | convolution fusion | flops 805314560 | bytes 6324224 | tf_op jit(solution)/shard_map/rka,abc->rkbc/dot_general | solution.py:51
  333.9 6.0 %fusion.60 = f32[2,32,64,256]{3,1,2,0:T(8,128)S(1)} fusion(f32[2,64,32,256]{3,1,2,0:T(8,128)S(1)} %pad_maximum_fusion.1, f32[1,32,2,32]{1,3,0,2:T(8,128)S(1)} %get-tuple-element.104, f32[1,32,2,32]{1,3,0,2:T(8,128)S(1)} %get-tuple-element.103), kind=kOutput, calls=%fused_computation.93 | convolution fusion | flops 805310464 | bytes 8404992 | tf_op jit(solution)/shard_map/rkbc,rbql->qlkc/dot_general | solution.py:59
  339.9 5.0 %multiply_add_fusion.3 = (f32[1,32,64,256]{3,1,2,0:T(8,128)}, f32[1,32,64,256]{3,1,2,0:T(8,128)}, f32[1,32,64,256]{3,1,2,0:T(8,128)}, f32[1,32,64,256]{3,1,2,0:T(8,128)}) fusion(f32[2,32,64,256]{3,1,2,0:T(8,128)S(1)} %copy-done.7, f32[2,32,64,256]{3,1,2,0:T(8,128)S(1)} %fusion.60, f32[2,32,64,256]{3,1,2,0:T(8,128)S(1)} %copy-done.1), kind=kLoop, calls=%fused_computation.154 | loop fusion | flops 6291456 | bytes 20971520 | tf_op jit(solution)/shard_map/add | solution.py:83
  347.5 6.2 %fusion.72 = f32[2,32,64,256]{3,1,2,0:T(8,128)S(1)} fusion(f32[2,64,32,256]{3,1,2,0:T(8,128)S(1)} %pad_maximum_fusion.7, f32[1,32,2,32]{1,3,0,2:T(8,128)S(1)} %get-tuple-element.104, f32[1,32,2,32]{1,3,0,2:T(8,128)S(1)} %get-tuple-element.103), kind=kOutput, calls=%fused_computation.97 | convolution fusion | flops 805310464 | bytes 8404992 | tf_op jit(solution)/shard_map/rkbc,rbql->qlkc/dot_general | solution.py:59
  353.7 5.2 %multiply_add_fusion.1 = (f32[1,32,64,256]{3,1,2,0:T(8,128)}, f32[1,32,64,256]{3,1,2,0:T(8,128)}, f32[1,32,64,256]{3,1,2,0:T(8,128)}, f32[1,32,64,256]{3,1,2,0:T(8,128)}) fusion(f32[2,32,64,256]{3,1,2,0:T(8,128)S(1)} %copy-done.5, f32[2,32,64,256]{3,1,2,0:T(8,128)S(1)} %fusion.72, f32[2,32,64,256]{3,1,2,0:T(8,128)S(1)} %copy-done.1), kind=kLoop, calls=%fused_computation.150 | loop fusion | flops 6291456 | bytes 20971520 | tf_op jit(solution)/shard_map/add | solution.py:83
  361.4 6.0 %fusion.66 = f32[2,32,64,256]{3,1,2,0:T(8,128)S(1)} fusion(f32[2,64,32,256]{3,1,2,0:T(8,128)S(1)} %pad_maximum_fusion.4, f32[1,32,2,32]{1,3,0,2:T(8,128)S(1)} %get-tuple-element.104, f32[1,32,2,32]{1,3,0,2:T(8,128)S(1)} %get-tuple-element.103), kind=kOutput, calls=%fused_computation.95 | convolution fusion | flops 805310464 | bytes 8404992 | tf_op jit(solution)/shard_map/rkbc,rbql->qlkc/dot_general | solution.py:59
  367.4 5.1 %multiply_add_fusion.2 = (f32[1,32,64,256]{3,1,2,0:T(8,128)}, f32[1,32,64,256]{3,1,2,0:T(8,128)}, f32[1,32,64,256]{3,1,2,0:T(8,128)}, f32[1,32,64,256]{3,1,2,0:T(8,128)}) fusion(f32[2,32,64,256]{3,1,2,0:T(8,128)S(1)} %copy-done.3, f32[2,32,64,256]{3,1,2,0:T(8,128)S(1)} %fusion.66, f32[2,32,64,256]{3,1,2,0:T(8,128)S(1)} %copy-done.1), kind=kLoop, calls=%fused_computation.152 | loop fusion | flops 6291456 | bytes 20971520 | tf_op jit(solution)/shard_map/add | solution.py:83
  372.5 6.0 %fusion.63 = f32[2,32,64,256]{3,1,2,0:T(8,128)S(1)} fusion(f32[1,32,64,256]{3,1,2,0:T(8,128)} %get-tuple-element.65, f32[1,32,64,256]{3,1,2,0:T(8,128)} %get-tuple-element.66, f32[1,32,2,32]{1,3,0,2:T(8,128)S(1)} %get-tuple-element.104, f32[1,32,2,32]{1,3,0,2:T(8,128)S(1)} %get-tuple-element.103), kind=kOutput, calls=%fused_computation.94 | convolution fusion | flops 806359040 | bytes 8404992 | tf_op jit(solution)/shard_map/qbrl,rlkc->qbkc/dot_general | solution.py:66
  390.7 6.3 %multiply_add_fusion = (f32[1,32,64,256]{3,1,2,0:T(8,128)}, f32[1,32,64,256]{3,1,2,0:T(8,128)}, f32[1,32,64,256]{3,1,2,0:T(8,128)}, f32[1,32,64,256]{3,1,2,0:T(8...) fusion(f32[2,32,64,256]{3,1,2,0:T(8,128)S(1)} %fusion.96, ...), kind=kLoop, calls=%fused_computation.148 | loop fusion | flops 12582912 | bytes 33570816 | tf_op jit(solution)/shard_map/add | solution.py:68
  421.4 11.7 %copy.406 = bf16[1,2048,256]{2,0,1:T(2,128)(2,1)S(1)} copy(bf16[1,2048,256]{2,1,0:T(8,128)(2,1)S(1)} %bitcast.320) | data formatting | bytes 2097152 | tf_op jit(solution)/shard_map/broadcast_in_dim | solution.py:123
  433.1 10.6 %reduce.3 = bf16[2048,256]{1,0:T(8,128)(2,1)S(1)} reduce(bf16[2048,1,256]{2,1,0:T(2,128)(2,1)S(1)} %bitcast.317, bf16[]{:T(256)} %broadcast.500), dimensions={1}, to_apply=%bitcast.299.reduce_sub_computation | reduce | bytes 2097154
  475.7 13.7 %reduce-scatter.2.cloned.1.call-done = bf16[128,256]{1,0:T(8,128)(2,1)} async-done(((bf16[1024,256]{1,0:T(8,128)(2,1)}), bf16[128,256]{1,0:T(8,128)(2,1)}) %reduce-scatter.2.cloned.1.call-update) | async-done | bytes 65552 | tf_op jit(solution)/shard_map/reduce_scatter | solution.py:136
  (182 shorter events, 173.9 us)
Async XLA Ops:
  9.6 17.3 %copy-start.12 = (bf16[1,128,4096]{1,2,0:T(8,128)(2,1)}, bf16[1,128,4096]{1,2,0:T(8,128)(2,1)S(1)}, u32[]{:S(2)}) copy-start(bf16[1,128,4096]{1,2,0:T(8,128)(2,1)S(1)} %copy.167) | copy-start | bytes 3145732
  50.9 10.2 %copy-start.44 = (s32[1,3]{1,0:T(1,128)S(1)}, s32[1,3]{1,0:T(1,128)}, u32[]{:S(2)}) copy-start(s32[1,3]{1,0:T(1,128)} %param.13) | copy-start | bytes 40
  50.9 10.6 %copy-start.40 = (f32[1024,256]{1,0:T(8,128)S(1)}, f32[1024,256]{1,0:T(8,128)}, u32[]{:S(2)}) copy-start(f32[1024,256]{1,0:T(8,128)} %param.11) | copy-start | bytes 3145732
  52.0 26.1 %all-to-all-start.2 = ((bf16[16,2,16384]{2,1,0:T(2,128)(2,1)}), bf16[16,2,16384]{2,1,0:T(2,128)(2,1)}, u32[]{:S(2)}, u32[]{:S(2)}) async-start(bf16[16,2,16384]{2,1,0:T(2,128)(2,1)} %reshape.446), calls=%async_computation.2 | async-start | bytes 2097152 | tf_op jit(solution)/shard_map/all_to_all | solution.py:130
  95.4 14.8 %copy-start.8 = (f32[2,64,32,256]{3,1,2,0:T(8,128)S(1)}, f32[2,64,32,256]{3,1,2,0:T(8,128)}, u32[]{:S(2)}) copy-start(f32[2,64,32,256]{3,1,2,0:T(8,128)} %fusion.125) | copy-start | bytes 12582916
  126.7 19.5 %copy-start.4 = (f32[2,32,64,256]{3,1,2,0:T(8,128)}, f32[2,32,64,256]{3,1,2,0:T(8,128)S(1)}, u32[]{:S(2)}) copy-start(f32[2,32,64,256]{3,1,2,0:T(8,128)S(1)} %fusion.90) | copy-start | bytes 12582916
  126.7 6.4 %copy-start.19 = (f32[1,64,32,256]{3,1,2,0:T(8,128)S(1)}, f32[1,64,32,256]{3,1,2,0:T(8,128)}, u32[]{:S(2)}) copy-start(f32[1,64,32,256]{3,1,2,0:T(8,128)} %get-tuple-element.90) | copy-start | bytes 6291460
  126.7 6.4 %copy-start.20 = (f32[1,64,32,256]{3,1,2,0:T(8,128)S(1)}, f32[1,64,32,256]{3,1,2,0:T(8,128)}, u32[]{:S(2)}) copy-start(f32[1,64,32,256]{3,1,2,0:T(8,128)} %get-tuple-element.91) | copy-start | bytes 6291460
  133.1 19.4 %copy-start = (f32[2,32,64,256]{3,1,2,0:T(8,128)}, f32[2,32,64,256]{3,1,2,0:T(8,128)S(1)}, u32[]{:S(2)}) copy-start(f32[2,32,64,256]{3,1,2,0:T(8,128)S(1)} %fusion.57) | copy-start | bytes 12582916
  133.6 6.0 %copy-start.18 = (f32[1,64,32,256]{3,1,2,0:T(8,128)S(1)}, f32[1,64,32,256]{3,1,2,0:T(8,128)}, u32[]{:S(2)}) copy-start(f32[1,64,32,256]{3,1,2,0:T(8,128)} %get-tuple-element.48) | copy-start | bytes 6291460
  139.6 12.9 %copy-start.2 = (f32[2,32,64,256]{3,1,2,0:T(8,128)}, f32[2,32,64,256]{3,1,2,0:T(8,128)S(1)}, u32[]{:S(2)}) copy-start(f32[2,32,64,256]{3,1,2,0:T(8,128)S(1)} %fusion.84) | copy-start | bytes 12582916
  146.2 6.3 %copy-start.6 = (f32[2,32,64,256]{3,1,2,0:T(8,128)}, f32[2,32,64,256]{3,1,2,0:T(8,128)S(1)}, u32[]{:S(2)}) copy-start(f32[2,32,64,256]{3,1,2,0:T(8,128)S(1)} %fusion.78) | copy-start | bytes 12582916
  157.6 5.6 %copy-start.27 = (f32[1,32,64,256]{3,1,2,0:T(8,128)S(1)}, f32[1,32,64,256]{3,1,2,0:T(8,128)}, u32[]{:S(2)}) copy-start(f32[1,32,64,256]{3,1,2,0:T(8,128)} %get-tuple-element.21) | copy-start | bytes 6291460
  157.6 5.6 %copy-start.28 = (f32[1,32,64,256]{3,1,2,0:T(8,128)S(1)}, f32[1,32,64,256]{3,1,2,0:T(8,128)}, u32[]{:S(2)}) copy-start(f32[1,32,64,256]{3,1,2,0:T(8,128)} %get-tuple-element.22) | copy-start | bytes 6291460
  213.5 6.9 %copy-start.41 = (bf16[1,128,4096]{2,1,0:T(8,128)(2,1)S(1)}, bf16[1,128,4096]{2,1,0:T(8,128)(2,1)}, u32[]{:S(2)}) copy-start(bf16[1,128,4096]{2,1,0:T(8,128)(2,1)} %param.8) | copy-start | bytes 3145732
  215.8 6.0 %copy-start.42 = (bf16[1,128,4096]{2,1,0:T(8,128)(2,1)S(1)}, bf16[1,128,4096]{2,1,0:T(8,128)(2,1)}, u32[]{:S(2)}) copy-start(bf16[1,128,4096]{2,1,0:T(8,128)(2,1)} %param.9) | copy-start | bytes 3145732
  215.8 20.6 %all-to-all-start.3 = ((bf16[16,2,16384]{2,1,0:T(2,128)(2,1)}), bf16[16,2,16384]{2,1,0:T(2,128)(2,1)}, u32[]{:S(2)}, u32[]{:S(2)}) async-start(bf16[16,2,16384]{2,1,0:T(2,128)(2,1)} %reshape.448), calls=%async_computation.3 | async-start | bytes 2097152 | tf_op jit(solution)/shard_map/all_to_all | solution.py:132
  333.9 6.0 %copy-start.1 = (f32[2,32,64,256]{3,1,2,0:T(8,128)S(1)}, f32[2,32,64,256]{3,1,2,0:T(8,128)}, u32[]{:S(2)}) copy-start(f32[2,32,64,256]{3,1,2,0:T(8,128)} %copy-done) | copy-start | bytes 12582916
  333.9 6.0 %copy-start.7 = (f32[2,32,64,256]{3,1,2,0:T(8,128)S(1)}, f32[2,32,64,256]{3,1,2,0:T(8,128)}, u32[]{:S(2)}) copy-start(f32[2,32,64,256]{3,1,2,0:T(8,128)} %copy-done.6) | copy-start | bytes 12582916
  347.5 6.2 %copy-start.5 = (f32[2,32,64,256]{3,1,2,0:T(8,128)S(1)}, f32[2,32,64,256]{3,1,2,0:T(8,128)}, u32[]{:S(2)}) copy-start(f32[2,32,64,256]{3,1,2,0:T(8,128)} %copy-done.4) | copy-start | bytes 12582916
  361.4 6.0 %copy-start.3 = (f32[2,32,64,256]{3,1,2,0:T(8,128)S(1)}, f32[2,32,64,256]{3,1,2,0:T(8,128)}, u32[]{:S(2)}) copy-start(f32[2,32,64,256]{3,1,2,0:T(8,128)} %copy-done.2) | copy-start | bytes 12582916
  372.5 6.0 %copy-start.16 = (f32[1,32,64,256]{3,1,2,0:T(8,128)S(1)}, f32[1,32,64,256]{3,1,2,0:T(8,128)}, u32[]{:S(2)}) copy-start(f32[1,32,64,256]{3,1,2,0:T(8,128)} %get-tuple-element.61) | copy-start | bytes 6291460
  372.5 6.0 %copy-start.17 = (f32[1,32,64,256]{3,1,2,0:T(8,128)S(1)}, f32[1,32,64,256]{3,1,2,0:T(8,128)}, u32[]{:S(2)}) copy-start(f32[1,32,64,256]{3,1,2,0:T(8,128)} %get-tuple-element.62) | copy-start | bytes 6291460
  378.5 8.1 %copy-start.33 = (f32[1,32,64,256]{3,1,2,0:T(8,128)S(1)}, f32[1,32,64,256]{3,1,2,0:T(8,128)}, u32[]{:S(2)}) copy-start(f32[1,32,64,256]{3,1,2,0:T(8,128)} %get-tuple-element.17) | copy-start | bytes 6291460
  378.5 8.1 %copy-start.34 = (f32[1,32,64,256]{3,1,2,0:T(8,128)S(1)}, f32[1,32,64,256]{3,1,2,0:T(8,128)}, u32[]{:S(2)}) copy-start(f32[1,32,64,256]{3,1,2,0:T(8,128)} %get-tuple-element.18) | copy-start | bytes 6291460
  382.5 4.1 copy-start.29
  382.6 4.1 copy-start.30
  382.6 4.1 copy-start.31
  382.6 4.1 copy-start.32
  443.7 5.1 %copy-start.14 = (f32[1,32,64,256]{3,1,2,0:T(8,128)S(1)}, f32[1,32,64,256]{3,1,2,0:T(8,128)}, u32[]{:S(2)}) copy-start(f32[1,32,64,256]{3,1,2,0:T(8,128)} %get-tuple-element.33) | copy-start | bytes 6291460
  444.8 17.9 %all-to-all-start.1 = ((bf16[16,2,16384]{2,1,0:T(2,128)(2,1)}), bf16[16,2,16384]{2,1,0:T(2,128)(2,1)S(1)}, u32[]{:S(2)}, u32[]{:S(2)}) async-start(bf16[16,2,16384]{2,1,0:T(2,128)(2,1)} %reshape.444), calls=%async_computation.1 | async-start | bytes 2097152 | tf_op jit(solution)/shard_map/all_to_all | solution.py:123
  448.5 40.9 %reduce-scatter.2.cloned.1.call-start = ((), (), s32[]{:S(2)}) async-start(), calls=%async_computation.5 | async-start | bytes 589824 | tf_op jit(solution)/shard_map/reduce_scatter | solution.py:136
  (17 other events, 42.9 us)
Sparse Core Ops, SparseCore 0:
  457.0 32.3 reduce-scatter.1
where the time goes:
time: 507 us; the launch traced here: 498 us
  matrix products  153 us (30%)
  other arithmetic  139 us (27%)
  local copies, waits for them, and re-layouts  114 us (22%)
  waiting for transfers between devices  40.9 us (8%)
  blocking collectives  18 us (4%)
  starting transfers between devices  17.1 us (3%)
  between operations  15.6 us (3%)
    unnamed x4, other arithmetic  69 us
    dot_general x7, matrix products, forward_dft(): jnp.einsum('rka,abc->rkbc', first, shaped, precision=lax.Precision.HIGHEST)  44.4 us
    dot_general x7, matrix products, forward_dft(): jnp.einsum('rkbc,rbql->qlkc', turned, second, precision=lax.Precision.HIG...  42.8 us
    unnamed x111, local copies, waits for them, and re-layouts  41.2 us
    dot_general x7, matrix products, inverse_dft(): jnp.einsum('aqk,qbkc->abc', back_first, turned, precision=lax.Precision.H...  33.4 us
    dot_general x7, matrix products, inverse_dft(): jnp.einsum('qbrl,rlkc->qbkc', second, spectral, precision=lax.Precision.H...  32.7 us
    add x5, other arithmetic, times_conj(): left[0] * right[0] + left[1] * right[1]  21.5 us
    all_to_all x1, blocking collectives, shards(): lax.all_to_all(product, 'ctx', split_axis=2, concat_axis=1, tiled=True)  18 us
  transfers between devices with their start and end apart: 4, of which 4 were waited for; matrix products, arithmetic and copies ran while one was open for 7% of the time, Pallas kernels for 0%

commit v1 on v0

v1 whole, which is shorter than its diff:
```python
import math

import jax
import jax.numpy as jnp
import numpy as np
from jax import lax
from jax.experimental import pallas as pl
from jax.experimental.pallas import tpu as pltpu
from jax.sharding import PartitionSpec as P

BLOCK = 256
VMEM = 56 * 1024 * 1024


def transform_tables(span, half):
    places = np.arange(span)
    doubled = (2 * np.arange(half)[:, None] + 1) * places[None, :] % (2 * span)
    angle = doubled * (math.pi / span)
    rows = np.concatenate([np.cos(angle), -np.sin(angle)], 0)
    into = rows.reshape(2 * half, span // BLOCK, BLOCK).transpose(1, 0, 2)
    back = (rows.T / half).reshape(span // BLOCK, BLOCK, 2 * half)
    return into.astype(jnp.bfloat16), back.astype(jnp.bfloat16)


def cost(flops, nbytes):
    return pl.CostEstimate(flops=flops, bytes_accessed=nbytes, transcendentals=0)


def params():
    return pltpu.CompilerParams(vmem_limit_bytes=VMEM)


def pair_kernel(left_ref, right_ref, out_ref):
    width = out_ref.shape[2]
    for part in range(out_ref.shape[0]):
        cols = slice(part * width, (part + 1) * width)
        left = left_ref[:, cols].astype(jnp.float32)
        right = right_ref[:, cols].astype(jnp.float32)
        out_ref[part] = (left * right).astype(jnp.bfloat16)


def pair_product(left, right, groups):
    rows, columns = left.shape
    width = columns // groups
    steps = 4
    per = groups // steps
    return pl.pallas_call(
        pair_kernel,
        grid=(steps,),
        in_specs=[pl.BlockSpec((rows, per * width), lambda i: (0, i))] * 2,
        out_specs=pl.BlockSpec((per, rows, width), lambda i: (i, 0, 0)),
        out_shape=jax.ShapeDtypeStruct((groups, rows, width), jnp.bfloat16),
        compiler_params=params(),
        cost_estimate=cost(rows * columns, 6 * rows * columns),
        name="pair_product",
    )(left, right)


def gate_kernel(inner_ref, first_ref, second_ref, one_ref, two_ref):
    width = inner_ref.shape[2]
    for part in range(inner_ref.shape[0]):
        cols = slice(part * width, (part + 1) * width)
        inner = inner_ref[part].astype(jnp.float32)
        one_ref[:, cols] = (inner * first_ref[:, cols].astype(jnp.float32)).astype(jnp.bfloat16)
        two_ref[:, cols] = (inner * second_ref[:, cols].astype(jnp.float32)).astype(jnp.bfloat16)


def gate_both(inner, first, second):
    groups, rows, width = inner.shape
    columns = groups * width
    steps = 4
    per = groups // steps
    flat = pl.BlockSpec((rows, per * width), lambda i: (0, i))
    return pl.pallas_call(
        gate_kernel,
        grid=(steps,),
        in_specs=[pl.BlockSpec((per, rows, width), lambda i: (i, 0, 0)), flat, flat],
        out_specs=[flat, flat],
        out_shape=[jax.ShapeDtypeStruct((rows, columns), jnp.bfloat16)] * 2,
        compiler_params=params(),
        cost_estimate=cost(2 * rows * columns, 10 * rows * columns),
        name="gate_both",
    )(inner, first, second)


def taps_kernel(taps_ref, into_ref, out_ref):
    step = pl.program_id(0)
    part = jnp.dot(
        into_ref[0], taps_ref[...].astype(jnp.bfloat16), preferred_element_type=jnp.float32
    )

    @pl.when(step == 0)
    def _():
        out_ref[...] = part

    @pl.when(step > 0)
    def _():
        out_ref[...] += part


def taps_spectrum(taps, into):
    reach, width = taps.shape
    size = into.shape[1]
    return pl.pallas_call(
        taps_kernel,
        grid=(reach // BLOCK,),
        in_specs=[
            pl.BlockSpec((BLOCK, width), lambda i: (i, 0)),
            pl.BlockSpec((1, size, BLOCK), lambda i: (i, 0, 0)),
        ],
        out_specs=pl.BlockSpec((size, width), lambda i: (0, 0)),
        out_shape=jax.ShapeDtypeStruct((size, width), jnp.float32),
        compiler_params=params(),
        cost_estimate=cost(2 * reach * size * width, 2 * reach * size + 4 * size * width),
        name="taps_spectrum",
    )(taps, into)


def window_ends(lengths_ref):
    first = lengths_ref[0, 0]
    second = first + lengths_ref[0, 1]
    return first, second


def window_of(place, ends):
    return (place >= ends[0]).astype(jnp.int32) + (place >= ends[1]).astype(jnp.int32)


def inside_window(window, base, shape, ends):
    places = base + lax.broadcasted_iota(jnp.int32, shape, 0)
    low = jnp.where(window == 0, 0, jnp.where(window == 1, ends[0], ends[1]))
    high = jnp.where(window == 0, ends[0], jnp.where(window == 1, ends[1], 1 << 30))
    return (places >= low) & (places < high)


def gather_spectra(block, ends, field_ref, into_ref, sums_ref):
    base = block * BLOCK
    field = field_ref[...].astype(jnp.float32)

    def one_window(window, carry):
        mask = inside_window(window, base, field.shape, ends)
        part = jnp.where(mask, field, 0.0).astype(jnp.bfloat16)
        sums_ref[window] += jnp.dot(into_ref[0], part, preferred_element_type=jnp.float32)
        return carry

    lax.fori_loop(window_of(base, ends), window_of(base + BLOCK - 1, ends) + 1, one_window, 0)


def scatter_back(block, ends, field_ref, gain_ref, back_ref, spectra_ref, total_ref, out_ref):
    base = block * BLOCK
    total_ref[...] = gain_ref[...] * field_ref[...].astype(jnp.float32)

    def one_window(window, carry):
        mask = inside_window(window, base, total_ref.shape, ends)
        part = jnp.dot(back_ref[0], spectra_ref[window], preferred_element_type=jnp.float32)
        total_ref[...] += jnp.where(mask, part, 0.0)
        return carry

    lax.fori_loop(window_of(base, ends), window_of(base + BLOCK - 1, ends) + 1, one_window, 0)
    out_ref[...] = total_ref[...].astype(jnp.bfloat16)


def forward_kernel(
    lengths_ref, field_ref, gain_ref, into_ref, back_ref, taps_any, out_ref, saved_any,
    sums_ref, taps_ref, spectra_ref, saved_ref, total_ref, sems,
):
    step = pl.program_id(0)
    blocks = pl.num_programs(0) // 2
    half = sums_ref.shape[1] // 2
    ends = window_ends(lengths_ref)
    taps_copy = pltpu.make_async_copy(taps_any, taps_ref, sems.at[0])
    saved_copy = pltpu.make_async_copy(saved_ref, saved_any, sems.at[1])

    @pl.when(step == 0)
    def _():
        taps_copy.start()
        sums_ref[...] = jnp.zeros_like(sums_ref)

    @pl.when(step < blocks)
    def _():
        gather_spectra(step, ends, field_ref, into_ref, sums_ref)

    @pl.when(step == blocks)
    def _():
        taps_copy.wait()

        def one_chunk(chunk, carry):
            low = pl.ds(pl.multiple_of(chunk * 64, 64), 64)
            high = pl.ds(pl.multiple_of(half + chunk * 64, 64), 64)
            tap_re, tap_im = taps_ref[low], taps_ref[high]
            for window in range(sums_ref.shape[0]):
                re, im = sums_ref[window, low], sums_ref[window, high]
                saved_ref[window, low] = re.astype(jnp.bfloat16)
                saved_ref[window, high] = im.astype(jnp.bfloat16)
                spectra_ref[window, low] = (tap_re * re - tap_im * im).astype(jnp.bfloat16)
                spectra_ref[window, high] = (tap_re * im + tap_im * re).astype(jnp.bfloat16)
            return carry

        lax.fori_loop(0, half // 64, one_chunk, 0)
        saved_copy.start()

    @pl.when(step >= blocks)
    def _():
        scatter_back(
            step - blocks, ends, field_ref, gain_ref, back_ref, spectra_ref, total_ref, out_ref
        )

    @pl.when(step == 2 * blocks - 1)
    def _():
        saved_copy.wait()


def conv_specs(blocks, size, width):
    return [
        pl.BlockSpec(memory_space=pltpu.SMEM),
        pl.BlockSpec((BLOCK, width), lambda i: (lax.rem(i, blocks), 0)),
        pl.BlockSpec((1, width), lambda i: (0, 0)),
        pl.BlockSpec((1, size, BLOCK), lambda i: (jnp.minimum(i, blocks - 1), 0, 0)),
        pl.BlockSpec((1, BLOCK, size), lambda i: (jnp.maximum(i - blocks, 0), 0, 0)),
    ]


def forward_mix(product, taps_spec, gain, lengths, into, back):
    rows, width = product.shape
    blocks, size, _ = into.shape
    windows = lengths.shape[1]
    return pl.pallas_call(
        forward_kernel,
        grid=(2 * blocks,),
        in_specs=conv_specs(blocks, size, width) + [pl.BlockSpec(memory_space=pl.ANY)],
        out_specs=[
            pl.BlockSpec((BLOCK, width), lambda i: (jnp.maximum(i - blocks, 0), 0)),
            pl.BlockSpec(memory_space=pl.ANY),
        ],
        out_shape=[
            jax.ShapeDtypeStruct((rows, width), jnp.bfloat16),
            jax.ShapeDtypeStruct((windows, size, width), jnp.bfloat16),
        ],
        scratch_shapes=[
            pltpu.VMEM((windows, size, width), jnp.float32),
            pltpu.VMEM((size, width), jnp.float32),
            pltpu.VMEM((windows, size, width), jnp.bfloat16),
            pltpu.VMEM((windows, size, width), jnp.bfloat16),
            pltpu.VMEM((BLOCK, width), jnp.float32),
            pltpu.SemaphoreType.DMA((2,)),
        ],
        compiler_params=params(),
        cost_estimate=cost(5 * rows * size * width, 4 * rows * size + 16 * size * width),
        name="forward_mix",
    )(lengths, product, gain, into, back, taps_spec)


def backward_kernel(
    lengths_ref, field_ref, gain_ref, into_ref, back_ref, taps_any, saved_any, out_ref, filter_ref,
    sums_ref, taps_ref, saved_ref, spectra_ref, cross_ref, total_ref, sems,
):
    step = pl.program_id(0)
    blocks = pl.num_programs(0) // 2
    half = sums_ref.shape[1] // 2
    ends = window_ends(lengths_ref)
    taps_copy = pltpu.make_async_copy(taps_any, taps_ref, sems.at[0])
    saved_copy = pltpu.make_async_copy(saved_any, saved_ref, sems.at[1])

    @pl.when(step == 0)
    def _():
        taps_copy.start()
        saved_copy.start()
        sums_ref[...] = jnp.zeros_like(sums_ref)

    @pl.when(step < blocks)
    def _():
        gather_spectra(step, ends, field_ref, into_ref, sums_ref)

    @pl.when(step == blocks)
    def _():
        taps_copy.wait()
        saved_copy.wait()

        def one_chunk(chunk, carry):
            low = pl.ds(pl.multiple_of(chunk * 64, 64), 64)
            high = pl.ds(pl.multiple_of(half + chunk * 64, 64), 64)
            tap_re, tap_im = taps_ref[low], taps_ref[high]
            cross_re = jnp.zeros(tap_re.shape, jnp.float32)
            cross_im = jnp.zeros(tap_re.shape, jnp.float32)
            for window in range(sums_ref.shape[0]):
                re, im = sums_ref[window, low], sums_ref[window, high]
                spectra_ref[window, low] = (tap_re * re + tap_im * im).astype(jnp.bfloat16)
                spectra_ref[window, high] = (tap_re * im - tap_im * re).astype(jnp.bfloat16)
                old_re = saved_ref[window, low].astype(jnp.float32)
                old_im = saved_ref[window, high].astype(jnp.float32)
                cross_re += re * old_re + im * old_im
                cross_im += im * old_re - re * old_im
            cross_ref[low] = cross_re.astype(jnp.bfloat16)
            cross_ref[high] = cross_im.astype(jnp.bfloat16)
            return carry

        lax.fori_loop(0, half // 64, one_chunk, 0)

    @pl.when((step >= blocks) & (step < blocks + blocks // 2))
    def _():
        part = jnp.dot(back_ref[0], cross_ref[...], preferred_element_type=jnp.float32)
        filter_ref[...] = part.astype(jnp.bfloat16)

    @pl.when(step >= blocks)
    def _():
        scatter_back(
            step - blocks, ends, field_ref, gain_ref, back_ref, spectra_ref, total_ref, out_ref
        )


def backward_mix(delta, taps_spec, saved, gain, lengths, into, back):
    rows, width = delta.shape
    blocks, size, _ = into.shape
    windows = lengths.shape[1]
    return pl.pallas_call(
        backward_kernel,
        grid=(2 * blocks,),
        in_specs=conv_specs(blocks, size, width) + [pl.BlockSpec(memory_space=pl.ANY)] * 2,
        out_specs=[
            pl.BlockSpec((BLOCK, width), lambda i: (jnp.maximum(i - blocks, 0), 0)),
            pl.BlockSpec(
                (BLOCK, width), lambda i: (jnp.clip(i - blocks, 0, blocks // 2 - 1), 0)
            ),
        ],
        out_shape=[
            jax.ShapeDtypeStruct((rows, width), jnp.bfloat16),
            jax.ShapeDtypeStruct((rows // 2, width), jnp.bfloat16),
        ],
        scratch_shapes=[
            pltpu.VMEM((windows, size, width), jnp.float32),
            pltpu.VMEM((size, width), jnp.float32),
            pltpu.VMEM((windows, size, width), jnp.bfloat16),
            pltpu.VMEM((windows, size, width), jnp.bfloat16),
            pltpu.VMEM((size, width), jnp.bfloat16),
            pltpu.VMEM((BLOCK, width), jnp.float32),
            pltpu.SemaphoreType.DMA((2,)),
        ],
        compiler_params=params(),
        cost_estimate=cost(6 * rows * size * width, 4 * rows * size + 16 * size * width),
        name="backward_mix",
    )(lengths, delta, gain, into, back, taps_spec, saved)


def swap(pieces):
    return lax.all_to_all(pieces, "ctx", split_axis=0, concat_axis=0, tiled=True)


def shards(queries, key_inputs, value_inputs, cotangent, filter_taps, skip_gain, lengths):
    groups = lax.axis_size("ctx")
    rows = queries.shape[1]
    total = rows * groups
    reach, width = filter_taps.shape
    into, back = transform_tables(total, reach)
    into, back = jnp.asarray(into), jnp.asarray(back)
    gain = skip_gain[None, :]
    product_cols = swap(pair_product(key_inputs[0], value_inputs[0], groups))
    delta_cols = swap(pair_product(cotangent[0], queries[0], groups))
    taps_spec = taps_spectrum(filter_taps, into)
    mixing, saved = forward_mix(
        product_cols.reshape(total, width), taps_spec, gain, lengths, into, back
    )
    mixing_rows = swap(mixing.reshape(groups, rows, width))
    units, filter_local = backward_mix(
        delta_cols.reshape(total, width), taps_spec, saved, gain, lengths, into, back
    )
    units_rows = swap(units.reshape(groups, rows, width))
    filter_grad = lax.psum_scatter(
        filter_local, "dp", scatter_dimension=0, tiled=True
    ).astype(jnp.float32) / lax.axis_size("dp")
    mixed_out, query_grad = gate_both(mixing_rows, queries[0], cotangent[0])
    key_grad, value_grad = gate_both(units_rows, value_inputs[0], key_inputs[0])
    return (mixed_out[None], query_grad[None], key_grad[None], value_grad[None], filter_grad)


def solution(mesh):
    rows_spec = P("dp", "ctx", None)
    in_specs = (rows_spec,) * 4 + (P(None, "ctx"), P("ctx"), P("dp", None))
    out_specs = (rows_spec,) * 4 + (P("dp", "ctx"),)
    return jax.shard_map(shards, mesh=mesh, in_specs=in_specs, out_specs=out_specs, check_vma=False)
```

time: 507 us -> 137 us (0.27); the launches traced: 498 us -> 135 us
  matrix products: 153 us -> 0 us
  other arithmetic: 139 us -> 1.5 us
  local copies, waits for them, and re-layouts: 114 us -> 0.99 us
  Pallas kernels: 0 us -> 63.2 us
  blocking collectives: 18 us -> 0 us
  waiting for transfers between devices: 40.9 us -> 29.3 us
  starting transfers between devices: 17.1 us -> 26.2 us
    dot_general x28 -> x0, matrix products: 153 us -> none  [the longest x7 44.4 us: forward_dft(): jnp.einsum('rka,abc->rkbc', first, shaped, precision=lax.Precision.HIGHEST)]
    unnamed x4 -> x0, other arithmetic: 69 us -> none
    pallas_call x0 -> x7, Pallas kernels: none -> 63.2 us  [the longest x1 21.6 us: backward_mix(): pl.pallas_call(backward_kernel, grid=(2 * blocks,), in_specs=conv_specs(b...]
    unnamed x111 -> x8, local copies, waits for them, and re-layouts: 41.2 us -> 0.99 us
    convert_element_type x2 -> x0, local copies, waits for them, and re-layouts: 33.7 us -> none  [the longest x1 17 us: shards(): delta = (cot_wide * query_wide).astype(jnp.bfloat16)]
    add x7 -> x0, other arithmetic: 29.9 us -> none  [the longest x5 21.5 us: times_conj(): left[0] * right[0] + left[1] * right[1]]
    broadcast_in_dim x2 -> x0, local copies, waits for them, and re-layouts: 23.5 us -> none  [the longest x1 11.7 us: shards(): units[None]]
    all_to_all x1 -> x0, blocking collectives: 18 us -> none  [shards(): lax.all_to_all(product, 'ctx', split_axis=2, concat_axis=1, tiled=True)]
  transfers between devices with their start and end apart: 4 -> 5, of which waited for: 4 -> 3; matrix products, arithmetic and copies ran while one was open for 7% -> 0% of each run, Pallas kernels for 0% -> 44%
where the time goes in v1:
time: 137 us; the launch traced here: 135 us
  Pallas kernels  63.2 us (46%)
  waiting for transfers between devices  29.3 us (21%)
  starting transfers between devices  26.2 us (19%)
  between operations  14.1 us (10%)
  other arithmetic  1.5 us (1%)
    all_to_all x4, starting transfers between devices, swap(): lax.all_to_all(pieces, 'ctx', split_axis=0, concat_axis=0, tiled=True)  26.2 us
    all_to_all x4, waiting for transfers between devices, swap(): lax.all_to_all(pieces, 'ctx', split_axis=0, concat_axis=0, tiled=True)  24.1 us
    pallas_call x1, Pallas kernels, backward_mix(): pl.pallas_call(backward_kernel, grid=(2 * blocks,), in_specs=conv_specs(b...  21.6 us
    pallas_call x1, Pallas kernels, forward_mix(): pl.pallas_call(forward_kernel, grid=(2 * blocks,), in_specs=conv_specs(bl...  20.1 us
    pallas_call x2, Pallas kernels, gate_both(): pl.pallas_call(gate_kernel, grid=(steps,), in_specs=[pl.BlockSpec((per, r...  8.11 us
    pallas_call x2, Pallas kernels, pair_product(): pl.pallas_call(pair_kernel, grid=(steps,), in_specs=[pl.BlockSpec((rows,...  7.28 us
    pallas_call x1, Pallas kernels, taps_spectrum(): pl.pallas_call(taps_kernel, grid=(reach // BLOCK,), in_specs=[pl.BlockSpe...  5.98 us
    reduce_scatter x1, waiting for transfers between devices, shards(): lax.psum_scatter(filter_local, 'dp', scatter_dimension=0, tiled=True)  5.14 us
  transfers between devices with their start and end apart: 5, of which 3 were waited for; matrix products, arithmetic and copies ran while one was open for 0% of the time, Pallas kernels for 44%

profile of v1, /device:TPU:0, one launch (start us, length us, event | category | flops | bytes accessed | tf_op | source)
XLA Modules:
  0.0 135.2 jit_solution(7529797820663435543)
XLA Ops:
  7.2 3.6 %pair_product.2 = bf16[16,128,256]{2,1,0:T(8,128)(2,1)} custom-call(bf16[128,4096]{1,0:T(8,128)(2,1)} %bitcast.17, bf16[128,4096]{1,0:T(8,128)(2,1)} %bitcast.19), custom_call_target="tpu_custom_call" | custom-call | flops 524288 | bytes 3145728 | tf_op jit(solution)/shard_map/pair_product/pallas_call | solution.py:47
  10.8 8.1 %all-to-all-start = ((bf16[16,128,256]{2,1,0:T(8,128)(2,1)}), bf16[16,128,256]{2,1,0:T(8,128)(2,1)S(1)}, u32[]{:S(2)}, u32[]{:S(2)}) async-start(bf16[16,128,256]{2,1,0:T(8,128)(2,1)} %pair_product.2), calls=%async_computation | async-start | bytes 2097152 | tf_op jit(solution)/shard_map/all_to_all | solution.py:345
  18.9 3.6 %pair_product.3 = bf16[16,128,256]{2,1,0:T(8,128)(2,1)} custom-call(bf16[128,4096]{1,0:T(8,128)(2,1)} %bitcast.15, bf16[128,4096]{1,0:T(8,128)(2,1)} %bitcast.13), custom_call_target="tpu_custom_call" | custom-call | flops 524288 | bytes 3145728 | tf_op jit(solution)/shard_map/pair_product/pallas_call | solution.py:47
  22.6 14.0 %all-to-all-done = bf16[16,128,256]{2,1,0:T(8,128)(2,1)S(1)} async-done(((bf16[16,128,256]{2,1,0:T(8,128)(2,1)}), bf16[16,128,256]{2,1,0:T(8,128)(2,1)S(1)}, u32[]{:S(2)}, u32[]{:S(2)}) %all-to-all-start) | async-done | bytes 1048608 | tf_op jit(solution)/shard_map/all_to_all | solution.py:345
  36.6 0.0 copy-start.1
  36.6 3.7 %all-to-all-start.2 = ((bf16[16,128,256]{2,1,0:T(8,128)(2,1)}), bf16[16,128,256]{2,1,0:T(8,128)(2,1)S(1)}, u32[]{:S(2)}, u32[]{:S(2)}) async-start(bf16[16,128,256]{2,1,0:T(8,128)(2,1)} %pair_product.3), calls=%async_computation.2 | async-start | bytes 2097152 | tf_op jit(solution)/shard_map/all_to_all | solution.py:345
  40.3 6.0 %taps_spectrum.1.taps_any = f32[2048,256]{1,0:T(8,128)} custom-call(f32[1024,256]{1,0:T(8,128)} %taps_ref.1, bf16[8,2048,256]{2,1,0:T(8,128)(2,1)} %constant.7.clone.into_ref), custom_call_target="tpu_custom_call" | custom-call | flops 1073741824 | bytes 6291456 | tf_op jit(solution)/shard_map/taps_spectrum/pallas_call | solution.py:104
  46.2 0.0 copy-done.1
  46.2 20.1 %forward_mix.1 = (bf16[2048,256]{1,0:T(8,128)(2,1)}, bf16[3,2048,256]{2,1,0:T(8,128)(2,1)}) custom-call(s32[1,3]{1,0:T(1,128)} %lengths_ref.3, bf16[2048,256]{1,0:T(8,128)(2,1)} %bitcast.21, f32[1,256]{1,0:T(1,128)} %bitcast.25, bf16[8,2048,256]{2,1,0:T(8,128)(2,1)} %constant.7.clone.into_ref, bf16[8,256,2048]{2,1,0:T(8,128)(2,1)} %constant.8.clone.back_ref, ...), custom_call_target="tpu_custom_call" | custom-call | flops 5368709120 | bytes 25165824 | tf_op jit(solution)/shard_map/forward_mix/pallas_call | solution.py:227
  66.4 0.0 all-to-all-done.2
  66.4 0.0 copy-start.3
  66.4 7.2 %all-to-all-start.1 = ((bf16[16,128,256]{2,1,0:T(8,128)(2,1)}), bf16[16,128,256]{2,1,0:T(8,128)(2,1)S(1)}, u32[]{:S(2)}, u32[]{:S(2)}) async-start(bf16[16,128,256]{2,1,0:T(8,128)(2,1)} %bitcast.22), calls=%async_computation.1 | async-start | bytes 2097152 | tf_op jit(solution)/shard_map/all_to_all | solution.py:345
  73.6 0.0 reduce-scatter.2.cloned.1.call-start
  73.6 0.0 copy-done.3
  73.6 21.6 %backward_mix.1 = (bf16[2048,256]{1,0:T(8,128)(2,1)}, bf16[1024,256]{1,0:T(8,128)(2,1)}) custom-call(s32[1,3]{1,0:T(1,128)} %lengths_ref.3, bf16[2048,256]{1,0:T(8,128)(2,1)} %bitcast.24, f32[1,256]{1,0:T(1,128)} %bitcast.26, bf16[8,2048,256]{2,1,0:T(8,128)(2,1)} %constant.7.clone.into_ref, bf16[8,256,2048]{2,1,0:T(8,128)(2,1)} %constant.8.clone.back_ref, ...), custom_call_target="tpu_custom_call" | custom-call | flops 6442450944 | bytes 25165824 | tf_op jit(solution)/shard_map/backward_mix/pallas_call | solution.py:315
  95.3 0.0 reduce-scatter.2.cloned.1.call-update
  95.3 0.0 all-to-all-done.1.inner_ref
  95.3 0.0 copy-start
  95.3 7.2 %all-to-all-start.3 = ((bf16[16,128,256]{2,1,0:T(8,128)(2,1)}), bf16[16,128,256]{2,1,0:T(8,128)(2,1)S(1)}, u32[]{:S(2)}, u32[]{:S(2)}) async-start(bf16[16,128,256]{2,1,0:T(8,128)(2,1)} %bitcast.23), calls=%async_computation.3 | async-start | bytes 2097152 | tf_op jit(solution)/shard_map/all_to_all | solution.py:345
  102.5 0.0 copy-done
  102.6 4.1 %gate_both.2 = (bf16[128,4096]{1,0:T(8,128)(2,1)}, bf16[128,4096]{1,0:T(8,128)(2,1)}) custom-call(bf16[16,128,256]{2,1,0:T(8,128)(2,1)} %copy-done, bf16[128,4096]{1,0:T(8,128)(2,1)} %bitcast.14, bf16[128,4096]{1,0:T(8,128)(2,1)} %bitcast.16), custom_call_target="tpu_custom_call" | custom-call | flops 1048576 | bytes 5242880 | tf_op jit(solution)/shard_map/gate_both/pallas_call | solution.py:74
  106.6 10.1 %all-to-all-done.3.inner_ref = bf16[16,128,256]{2,1,0:T(8,128)(2,1)S(1)} async-done(((bf16[16,128,256]{2,1,0:T(8,128)(2,1)}), bf16[16,128,256]{2,1,0:T(8,128)(2,1)S(1)}, u32[]{:S(2)}, u32[]{:S(2)}) %all-to-all-start.3) | async-done | bytes 1048608 | tf_op jit(solution)/shard_map/all_to_all | solution.py:345
  116.7 0.0 copy-start.2
  116.7 1.0 copy-done.2
  117.7 4.0 %gate_both.3 = (bf16[128,4096]{1,0:T(8,128)(2,1)}, bf16[128,4096]{1,0:T(8,128)(2,1)}) custom-call(bf16[16,128,256]{2,1,0:T(8,128)(2,1)} %copy-done.2, bf16[128,4096]{1,0:T(8,128)(2,1)} %bitcast.20, bf16[128,4096]{1,0:T(8,128)(2,1)} %bitcast.18), custom_call_target="tpu_custom_call" | custom-call | flops 1048576 | bytes 5242880 | tf_op jit(solution)/shard_map/gate_both/pallas_call | solution.py:74
  121.8 5.1 %reduce-scatter.2.cloned.1.call-done = bf16[128,256]{1,0:T(8,128)(2,1)} async-done(((bf16[1024,256]{1,0:T(8,128)(2,1)}), bf16[128,256]{1,0:T(8,128)(2,1)}) %reduce-scatter.2.cloned.1.call-update) | async-done | bytes 65552 | tf_op jit(solution)/shard_map/reduce_scatter | solution.py:367
  126.9 1.5 %convert_multiply_fusion = f32[128,256]{1,0:T(8,128)} fusion(bf16[128,256]{1,0:T(8,128)(2,1)} %reduce-scatter.2.cloned.1.call-done), kind=kLoop, calls=%fused_computation | loop fusion | flops 65536 | bytes 196608 | tf_op jit(solution)/shard_map/div | solution.py:367
Async XLA Ops:
  10.8 25.8 %all-to-all-start = ((bf16[16,128,256]{2,1,0:T(8,128)(2,1)}), bf16[16,128,256]{2,1,0:T(8,128)(2,1)S(1)}, u32[]{:S(2)}, u32[]{:S(2)}) async-start(bf16[16,128,256]{2,1,0:T(8,128)(2,1)} %pair_product.2), calls=%async_computation | async-start | bytes 2097152 | tf_op jit(solution)/shard_map/all_to_all | solution.py:345
  36.6 9.7 %copy-start.1 = (bf16[16,128,256]{2,1,0:T(8,128)(2,1)}, bf16[16,128,256]{2,1,0:T(8,128)(2,1)S(1)}, u32[]{:S(2)}) copy-start(bf16[16,128,256]{2,1,0:T(8,128)(2,1)S(1)} %all-to-all-done) | copy-start | bytes 3145732
  36.6 29.8 %all-to-all-start.2 = ((bf16[16,128,256]{2,1,0:T(8,128)(2,1)}), bf16[16,128,256]{2,1,0:T(8,128)(2,1)S(1)}, u32[]{:S(2)}, u32[]{:S(2)}) async-start(bf16[16,128,256]{2,1,0:T(8,128)(2,1)} %pair_product.3), calls=%async_computation.2 | async-start | bytes 2097152 | tf_op jit(solution)/shard_map/all_to_all | solution.py:345
  66.4 7.2 %copy-start.3 = (bf16[16,128,256]{2,1,0:T(8,128)(2,1)}, bf16[16,128,256]{2,1,0:T(8,128)(2,1)S(1)}, u32[]{:S(2)}) copy-start(bf16[16,128,256]{2,1,0:T(8,128)(2,1)S(1)} %all-to-all-done.2) | copy-start | bytes 3145732
  66.4 28.9 %all-to-all-start.1 = ((bf16[16,128,256]{2,1,0:T(8,128)(2,1)}), bf16[16,128,256]{2,1,0:T(8,128)(2,1)S(1)}, u32[]{:S(2)}, u32[]{:S(2)}) async-start(bf16[16,128,256]{2,1,0:T(8,128)(2,1)} %bitcast.22), calls=%async_computation.1 | async-start | bytes 2097152 | tf_op jit(solution)/shard_map/all_to_all | solution.py:345
  73.6 53.3 %reduce-scatter.2.cloned.1.call-start = ((), (), s32[]{:S(2)}) async-start(), calls=%async_computation.5 | async-start | bytes 589824 | tf_op jit(solution)/shard_map/reduce_scatter | solution.py:367
  95.3 7.2 %copy-start = (bf16[16,128,256]{2,1,0:T(8,128)(2,1)}, bf16[16,128,256]{2,1,0:T(8,128)(2,1)S(1)}, u32[]{:S(2)}) copy-start(bf16[16,128,256]{2,1,0:T(8,128)(2,1)S(1)} %all-to-all-done.1.inner_ref) | copy-start | bytes 3145732
  95.3 21.4 %all-to-all-start.3 = ((bf16[16,128,256]{2,1,0:T(8,128)(2,1)}), bf16[16,128,256]{2,1,0:T(8,128)(2,1)S(1)}, u32[]{:S(2)}, u32[]{:S(2)}) async-start(bf16[16,128,256]{2,1,0:T(8,128)(2,1)} %bitcast.23), calls=%async_computation.3 | async-start | bytes 2097152 | tf_op jit(solution)/shard_map/all_to_all | solution.py:345
  116.7 1.0 copy-start.2
Sparse Core Ops, SparseCore 0:
  95.4 31.4 reduce-scatter.1

commit v2 on v0

v2 whole, which is shorter than its diff:
```python
import math

import jax
import jax.numpy as jnp
import numpy as np
from jax import lax
from jax.experimental import pallas as pl
from jax.experimental.pallas import tpu as pltpu
from jax.sharding import PartitionSpec as P

MIB = 1024 * 1024
LANES = 128
TILE = 256
STRIP = 512
FAR = pl.BlockSpec(memory_space=pltpu.HBM)
SCALARS = pl.BlockSpec(memory_space=pltpu.SMEM)
LOCAL = pl.BlockSpec(memory_space=pltpu.VMEM)


def transform_tables(reach):
    places = np.arange(reach)
    doubled = (2 * np.arange(reach)[:, None] + 1) * places[None, :] % (4 * reach)
    angle = doubled * (math.pi / (2 * reach))
    rows = np.stack([np.cos(angle), -np.sin(angle)], 0)
    rows = rows.reshape(2, 2 * reach // TILE, TILE // 2, reach).transpose(1, 0, 2, 3)
    rows = rows.reshape(2 * reach, reach)
    return rows.astype(jnp.bfloat16), (rows.T / reach).astype(jnp.bfloat16)


def cost(flops, nbytes):
    return pl.CostEstimate(flops=flops, bytes_accessed=nbytes, transcendentals=0)


def far(array):
    return pltpu.with_memory_space_constraint(array, pltpu.HBM)


def near(array):
    return pltpu.with_memory_space_constraint(array, pltpu.VMEM)


def params(mebibytes):
    return pltpu.CompilerParams(vmem_limit_bytes=mebibytes * MIB)


def pair_kernel(left_any, right_any, out_any, left_ref, right_ref, out_ref, sems):
    width = out_ref.shape[2]
    chunks = sems.shape[1]
    per = out_ref.shape[0] // chunks
    loads = []
    for chunk in range(chunks):
        cols = pl.ds(chunk * per * width, per * width)
        for index, (source, held) in enumerate(((left_any, left_ref), (right_any, right_ref))):
            copy = pltpu.make_async_copy(
                source.at[:, cols], held.at[:, cols], sems.at[index, chunk]
            )
            copy.start()
            loads.append(copy)
    stores = []
    for chunk in range(chunks):
        loads[2 * chunk].wait()
        loads[2 * chunk + 1].wait()
        for part in range(chunk * per, (chunk + 1) * per):
            cols = slice(part * width, (part + 1) * width)
            left = left_ref[:, cols].astype(jnp.float32)
            right = right_ref[:, cols].astype(jnp.float32)
            out_ref[part] = (left * right).astype(jnp.bfloat16)
        rows = pl.ds(chunk * per, per)
        copy = pltpu.make_async_copy(out_ref.at[rows], out_any.at[rows], sems.at[2, chunk])
        copy.start()
        stores.append(copy)
    for copy in stores:
        copy.wait()


def pair_product(left, right, groups):
    rows, columns = left.shape
    shape = (groups, rows, columns // groups)
    return pl.pallas_call(
        pair_kernel,
        in_specs=[FAR] * 2,
        out_specs=FAR,
        out_shape=pltpu.HBM(shape, jnp.bfloat16),
        scratch_shapes=[
            pltpu.VMEM((rows, columns), jnp.bfloat16),
            pltpu.VMEM((rows, columns), jnp.bfloat16),
            pltpu.VMEM(shape, jnp.bfloat16),
            pltpu.SemaphoreType.DMA((3, 4)),
        ],
        compiler_params=params(8),
        cost_estimate=cost(rows * columns, 6 * rows * columns),
        name="pair_product",
    )(far(left), far(right))


def gate_kernel(
    inner_any, first_any, second_any, ahead_any, one_any, two_any, ahead_out,
    inner_ref, first_ref, second_ref, one_ref, two_ref, sems, hold_sem,
):
    groups, _, width = inner_ref.shape
    chunks = sems.shape[1]
    per = groups // chunks
    loads, stores = [], []
    for chunk in range(chunks):
        rows = pl.ds(chunk * per, per)
        cols = pl.ds(chunk * per * width, per * width)
        for copy in (
            pltpu.make_async_copy(inner_any.at[rows], inner_ref.at[rows], sems.at[0, chunk]),
            pltpu.make_async_copy(first_any.at[:, cols], first_ref.at[:, cols], sems.at[1, chunk]),
            pltpu.make_async_copy(second_any.at[:, cols], second_ref.at[:, cols], sems.at[2, chunk]),
        ):
            copy.start()
            loads.append(copy)
    copy = pltpu.make_async_copy(ahead_any, ahead_out, hold_sem)
    copy.start()
    stores.append(copy)
    for chunk in range(chunks):
        for copy in loads[3 * chunk : 3 * chunk + 3]:
            copy.wait()
        for part in range(chunk * per, (chunk + 1) * per):
            cols = slice(part * width, (part + 1) * width)
            inner = inner_ref[part].astype(jnp.float32)
            one_ref[:, cols] = (inner * first_ref[:, cols].astype(jnp.float32)).astype(jnp.bfloat16)
            two_ref[:, cols] = (inner * second_ref[:, cols].astype(jnp.float32)).astype(
                jnp.bfloat16
            )
        cols = pl.ds(chunk * per * width, per * width)
        for index, (held, target) in enumerate(((one_ref, one_any), (two_ref, two_any))):
            copy = pltpu.make_async_copy(
                held.at[:, cols], target.at[:, cols], sems.at[3 + index, chunk]
            )
            copy.start()
            stores.append(copy)
    for copy in stores:
        copy.wait()


def gate_both(inner, first, second, ahead):
    groups, rows, width = inner.shape
    columns = groups * width
    held = pltpu.VMEM((rows, columns), jnp.bfloat16)
    return pl.pallas_call(
        gate_kernel,
        in_specs=[pl.BlockSpec(memory_space=pl.ANY)] + [FAR] * 3,
        out_specs=[FAR] * 2 + [LOCAL],
        out_shape=[pltpu.HBM((rows, columns), jnp.bfloat16)] * 2 + [held],
        scratch_shapes=[
            pltpu.VMEM((groups, rows, width), jnp.bfloat16),
            held, held, held, held,
            pltpu.SemaphoreType.DMA((5, 4)),
            pltpu.SemaphoreType.DMA,
        ],
        compiler_params=params(12),
        cost_estimate=cost(2 * rows * columns, 12 * rows * columns),
        name="gate_both",
    )(inner, far(first), far(second), far(ahead))


def last_kernel(
    inner_ref, first_any, second_ref, one_any, two_any, first_ref, one_ref, two_ref, sems
):
    groups, _, width = inner_ref.shape
    chunks = sems.shape[1]
    per = groups // chunks
    loads, stores = [], []
    for chunk in range(chunks):
        cols = pl.ds(chunk * per * width, per * width)
        copy = pltpu.make_async_copy(first_any.at[:, cols], first_ref.at[:, cols], sems.at[2, chunk])
        copy.start()
        loads.append(copy)
    for chunk in range(chunks):
        loads[chunk].wait()
        for part in range(chunk * per, (chunk + 1) * per):
            cols = slice(part * width, (part + 1) * width)
            inner = inner_ref[part].astype(jnp.float32)
            one_ref[:, cols] = (inner * first_ref[:, cols].astype(jnp.float32)).astype(jnp.bfloat16)
            two_ref[:, cols] = (inner * second_ref[:, cols].astype(jnp.float32)).astype(
                jnp.bfloat16
            )
        cols = pl.ds(chunk * per * width, per * width)
        for index, (held, target) in enumerate(((one_ref, one_any), (two_ref, two_any))):
            copy = pltpu.make_async_copy(held.at[:, cols], target.at[:, cols], sems.at[index, chunk])
            copy.start()
            stores.append(copy)
    for copy in stores:
        copy.wait()


def gate_last(inner, first, second):
    groups, rows, width = inner.shape
    columns = groups * width
    held = pltpu.VMEM((rows, columns), jnp.bfloat16)
    return pl.pallas_call(
        last_kernel,
        in_specs=[LOCAL, FAR, LOCAL],
        out_specs=[FAR] * 2,
        out_shape=[pltpu.HBM((rows, columns), jnp.bfloat16)] * 2,
        scratch_shapes=[held, held, held, pltpu.SemaphoreType.DMA((3, 4))],
        compiler_params=params(8),
        cost_estimate=cost(2 * rows * columns, 10 * rows * columns),
        name="gate_last",
    )(near(inner), far(first), near(second))


def taps_kernel(taps_any, into_any, out_any, taps_ref, into_ref, out_ref, sems):
    size = out_ref.shape[0]
    tiles = size // TILE
    first = pltpu.make_async_copy(taps_any, taps_ref, sems.at[0, 0])
    first.start()
    loads, stores = [], []
    for tile in range(tiles):
        rows = pl.ds(tile * TILE, TILE)
        copy = pltpu.make_async_copy(into_any.at[rows], into_ref.at[rows], sems.at[1, tile])
        copy.start()
        loads.append(copy)
    first.wait()
    taps = taps_ref[...].astype(jnp.bfloat16)
    for tile in range(tiles):
        rows = slice(tile * TILE, (tile + 1) * TILE)
        loads[tile].wait()
        part = jnp.dot(into_ref[rows], taps, preferred_element_type=jnp.float32)
        out_ref[rows] = part.astype(jnp.bfloat16)
        rows = pl.ds(tile * TILE, TILE)
        copy = pltpu.make_async_copy(out_ref.at[rows], out_any.at[rows], sems.at[2, tile])
        copy.start()
        stores.append(copy)
    for copy in stores:
        copy.wait()


def taps_spectrum(taps, into):
    reach, width = taps.shape
    size = into.shape[0]
    return pl.pallas_call(
        taps_kernel,
        in_specs=[FAR] * 2,
        out_specs=FAR,
        out_shape=pltpu.HBM((size, width), jnp.bfloat16),
        scratch_shapes=[
            pltpu.VMEM((reach, width), jnp.float32),
            pltpu.VMEM((size, reach), jnp.bfloat16),
            pltpu.VMEM((size, width), jnp.bfloat16),
            pltpu.SemaphoreType.DMA((3, size // TILE)),
        ],
        compiler_params=params(12),
        cost_estimate=cost(2 * reach * size * width, 2 * reach * size + 4 * size * width),
        name="taps_spectrum",
    )(far(taps), far(into))


def window_order(lengths_ref):
    lengths = [lengths_ref[0, window] for window in range(3)]
    starts = [jnp.int32(0), lengths[0], lengths[0] + lengths[1]]
    first = (lengths[0] >= lengths[1]) & (lengths[0] >= lengths[2])
    second = ~first & (lengths[1] >= lengths[2])
    longest = jnp.where(first, 0, jnp.where(second, 1, 2))
    low = jnp.where(longest == 0, 1, 0)
    high = jnp.where(longest == 2, 1, 2)
    pick = lambda values, index: jnp.where(
        index == 0, values[0], jnp.where(index == 1, values[1], values[2])
    )
    swapped = pick(lengths, low) < pick(lengths, high)
    middle = jnp.where(swapped, high, low)
    shortest = jnp.where(swapped, low, high)
    slots = [(pick(starts, index), pick(lengths, index)) for index in (longest, middle, shortest)]
    places = [
        (
            jnp.where(longest == window, 0, jnp.where(middle == window, 1, 2)),
            starts[window],
            lengths[window],
        )
        for window in range(3)
    ]
    return slots, places


def spread(field_ref, wide_ref):
    rows = field_ref.shape[0]
    for half in range(wide_ref.shape[0]):
        lanes = slice(half * LANES, (half + 1) * LANES)
        wide_ref[half, :rows] = field_ref[:, lanes].astype(jnp.float32)


def take_windows(wide_ref, part_ref, slots):
    reach = part_ref.shape[0]
    for slot, (start, length) in enumerate(slots):
        rows = reach // 2 if slot == 2 else reach
        inside = lax.broadcasted_iota(jnp.int32, (rows, LANES), 0) < length
        for half in range(wide_ref.shape[0]):
            lane = (slot * wide_ref.shape[0] + half) * LANES
            part = jnp.where(inside, wide_ref[half, pl.ds(start, rows)], 0.0)
            part_ref[:rows, lane : lane + LANES] = part.astype(jnp.bfloat16)


def transform_rows(into_ref, part_ref, low, width):
    reach = part_ref.shape[0]
    rows = slice(low, low + TILE)
    long = jnp.dot(into_ref[rows], part_ref[:, : 2 * width], preferred_element_type=jnp.float32)
    short = jnp.dot(
        into_ref[rows, : reach // 2],
        part_ref[: reach // 2, 2 * width :],
        preferred_element_type=jnp.float32,
    )
    return long[:, :width], long[:, width:], short


def place_windows(held_ref, wide_ref, places):
    reach = held_ref.shape[2]
    for slot, start, length in places:

        def body(rows):
            for half in range(wide_ref.shape[0]):
                wide_ref[half, pl.ds(start, rows)] = held_ref[slot, half, :rows]

        @pl.when(length > reach // 2)
        def _():
            body(reach)

        @pl.when(length <= reach // 2)
        def _():
            body(reach // 2)


def hold_rows(held_ref, slot, low, part):
    for half in range(held_ref.shape[1]):
        lanes = slice(half * LANES, (half + 1) * LANES)
        held_ref[slot, half, low : low + part.shape[0]] = part[:, lanes]


def finish(field_ref, gain_ref, wide_ref, out_ref, out_any, sem):
    rows = out_ref.shape[0]
    step = rows // sem.shape[0]
    copies = []
    for index in range(sem.shape[0]):
        place = slice(index * step, (index + 1) * step)
        for half in range(wide_ref.shape[0]):
            lanes = slice(half * LANES, (half + 1) * LANES)
            direct = gain_ref[:, lanes] * field_ref[place, lanes].astype(jnp.float32)
            out_ref[place, lanes] = (wide_ref[half, place] + direct).astype(jnp.bfloat16)
        place = pl.ds(index * step, step)
        copy = pltpu.make_async_copy(out_ref.at[place], out_any.at[place], sem.at[index])
        copy.start()
        copies.append(copy)
    for copy in copies:
        copy.wait()


def copy_parts(source, held, sems):
    parts = sems.shape[0]
    step = source.shape[0] // parts
    copies = []
    for part in range(parts):
        rows = pl.ds(part * step, step)
        copies.append(pltpu.make_async_copy(source.at[rows], held.at[rows], sems.at[part]))
    return copies


def begin(copies):
    for copy in copies:
        copy.start()


def finished(copies):
    for copy in copies:
        copy.wait()


def forward_kernel(
    lengths_ref, field_any, gain_ref, into_any, back_any, taps_any, out_any, saved_any,
    field_ref, into_ref, back_ref, taps_ref, out_ref, saved_ref,
    part_ref, spectra_ref, held_ref, wide_ref, sems, load_sems, out_sems,
):
    size, reach = into_ref.shape
    width = taps_ref.shape[1]
    parts = load_sems.shape[1]
    field_copy = pltpu.make_async_copy(field_any, field_ref, sems.at[0])
    back_copy = pltpu.make_async_copy(back_any, back_ref, sems.at[1])
    into_copies = copy_parts(into_any, into_ref, load_sems.at[0])
    taps_copies = copy_parts(taps_any, taps_ref, load_sems.at[1])
    saved_copies = copy_parts(saved_ref, saved_any, load_sems.at[2])
    stages = [list(copies) for copies in zip(into_copies, taps_copies)]
    begin([field_copy] + stages[0])
    slots, places = window_order(lengths_ref)
    field_copy.wait()
    begin(stages[1] + stages[2])
    spread(field_ref, wide_ref)
    take_windows(wide_ref, part_ref, slots)
    for low in range(0, size, TILE):
        part, start = divmod(low * parts, size)
        if start == 0:
            finished(stages[part])
            begin({0: stages[3], 1: [back_copy]}.get(part, []))
        mid, high = low + TILE // 2, low + TILE
        tap_re = taps_ref[low:mid].astype(jnp.float32)
        tap_im = taps_ref[mid:high].astype(jnp.float32)
        for slot, both in enumerate(transform_rows(into_ref, part_ref, low, width)):
            lanes = slice(slot * width, (slot + 1) * width)
            re, im = both[: TILE // 2], both[TILE // 2 :]
            saved_ref[low:high, lanes] = both.astype(jnp.bfloat16)
            spectra_ref[low:mid, lanes] = (tap_re * re - tap_im * im).astype(jnp.bfloat16)
            spectra_ref[mid:high, lanes] = (tap_re * im + tap_im * re).astype(jnp.bfloat16)
        if start + TILE * parts == size:
            begin([saved_copies[part]])
    back_copy.wait()
    for low in range(0, reach, STRIP):
        long = jnp.dot(
            back_ref[low : low + STRIP],
            spectra_ref[:, : 2 * width],
            preferred_element_type=jnp.float32,
        )
        hold_rows(held_ref, 0, low, long[:, :width])
        hold_rows(held_ref, 1, low, long[:, width:])
    short = jnp.dot(
        back_ref[: reach // 2], spectra_ref[:, 2 * width :], preferred_element_type=jnp.float32
    )
    hold_rows(held_ref, 2, 0, short)
    place_windows(held_ref, wide_ref, places)
    finish(field_ref, gain_ref, wide_ref, out_ref, out_any, out_sems)
    finished(saved_copies)


def forward_mix(product, taps_spec, gain, lengths, into, back):
    rows, width = product.shape
    size, reach = into.shape
    windows = lengths.shape[1]
    return pl.pallas_call(
        forward_kernel,
        in_specs=[SCALARS, FAR, LOCAL, FAR, FAR, FAR],
        out_specs=[FAR] * 2,
        out_shape=[
            pltpu.HBM((rows, width), jnp.bfloat16),
            pltpu.HBM((size, windows * width), jnp.bfloat16),
        ],
        scratch_shapes=[
            pltpu.VMEM((rows, width), jnp.bfloat16),
            pltpu.VMEM((size, reach), jnp.bfloat16),
            pltpu.VMEM((reach, size), jnp.bfloat16),
            pltpu.VMEM((size, width), jnp.bfloat16),
            pltpu.VMEM((rows, width), jnp.bfloat16),
            pltpu.VMEM((size, windows * width), jnp.bfloat16),
            pltpu.VMEM((reach, windows * width), jnp.bfloat16),
            pltpu.VMEM((size, windows * width), jnp.bfloat16),
            pltpu.VMEM((windows, width // LANES, reach, LANES), jnp.float32),
            pltpu.VMEM((width // LANES, rows + reach // 2, LANES), jnp.float32),
            pltpu.SemaphoreType.DMA((2,)),
            pltpu.SemaphoreType.DMA((3, 4)),
            pltpu.SemaphoreType.DMA((4,)),
        ],
        compiler_params=params(40),
        cost_estimate=cost(6 * rows * size * width, 4 * rows * size + 16 * size * width),
        name="forward_mix",
    )(lengths, far(product), gain, far(into), far(back), far(taps_spec))


def backward_kernel(
    lengths_ref, place_ref, field_any, gain_ref, into_any, back_any, taps_any, saved_any,
    out_any, kept_any, away_any,
    field_ref, into_ref, back_ref, taps_ref, out_ref, saved_ref, filter_ref,
    part_ref, spectra_ref, held_ref, wide_ref, sems, load_sems, filter_sems, out_sems,
):
    size, reach = into_ref.shape
    width = taps_ref.shape[1]
    parts = load_sems.shape[1]
    field_copy = pltpu.make_async_copy(field_any, field_ref, sems.at[0])
    back_copy = pltpu.make_async_copy(back_any, back_ref, sems.at[1])
    into_copies = copy_parts(into_any, into_ref, load_sems.at[0])
    taps_copies = copy_parts(taps_any, taps_ref, load_sems.at[1])
    saved_copies = copy_parts(saved_any, saved_ref, load_sems.at[2])
    stages = [list(copies) for copies in zip(into_copies, taps_copies, saved_copies)]
    begin([field_copy] + stages[0])
    slots, places = window_order(lengths_ref)
    field_copy.wait()
    begin(stages[1] + stages[2])
    spread(field_ref, wide_ref)
    take_windows(wide_ref, part_ref, slots)
    for low in range(0, size, TILE):
        part, start = divmod(low * parts, size)
        if start == 0:
            finished(stages[part])
            begin({0: stages[3], 1: [back_copy]}.get(part, []))
        mid, high = low + TILE // 2, low + TILE
        tap_re = taps_ref[low:mid].astype(jnp.float32)
        tap_im = taps_ref[mid:high].astype(jnp.float32)
        cross_re, cross_im = 0.0, 0.0
        for slot, both in enumerate(transform_rows(into_ref, part_ref, low, width)):
            lanes = slice(slot * width, (slot + 1) * width)
            re, im = both[: TILE // 2], both[TILE // 2 :]
            spectra_ref[low:mid, lanes] = (tap_re * re + tap_im * im).astype(jnp.bfloat16)
            spectra_ref[mid:high, lanes] = (tap_re * im - tap_im * re).astype(jnp.bfloat16)
            old_re = saved_ref[low:mid, lanes].astype(jnp.float32)
            old_im = saved_ref[mid:high, lanes].astype(jnp.float32)
            cross_re += re * old_re + im * old_im
            cross_im += im * old_re - re * old_im
        spectra_ref[low:mid, 3 * width :] = cross_re.astype(jnp.bfloat16)
        spectra_ref[mid:high, 3 * width :] = cross_im.astype(jnp.bfloat16)
    back_copy.wait()
    for low in range(0, reach, STRIP):
        rows = slice(low, low + STRIP)
        if low < reach // 2:
            short = jnp.dot(
                back_ref[rows], spectra_ref[:, 2 * width :], preferred_element_type=jnp.float32
            )
            hold_rows(held_ref, 2, low, short[:, :width])
            terms = short[:, width:]
        else:
            terms = jnp.dot(
                back_ref[rows], spectra_ref[:, 3 * width :], preferred_element_type=jnp.float32
            )
        filter_ref[rows] = terms.astype(jnp.bfloat16)

    count, height, _ = kept_any.shape
    core, chip = place_ref[0] % 2, place_ref[0] // 2

    def each_block(act):
        for block in range(2 * count):
            rows = pl.ds(block * height, height)
            for same, target in ((0, kept_any), (1, away_any)):

                @pl.when((core + block) % 2 == same)
                def _():
                    act(
                        pltpu.make_async_copy(
                            filter_ref.at[rows], target.at[(block // 2) ^ chip],
                            filter_sems.at[block],
                        )
                    )

    each_block(lambda copy: copy.start())
    for low in range(0, reach, STRIP):
        long = jnp.dot(
            back_ref[low : low + STRIP],
            spectra_ref[:, : 2 * width],
            preferred_element_type=jnp.float32,
        )
        hold_rows(held_ref, 0, low, long[:, :width])
        hold_rows(held_ref, 1, low, long[:, width:])
    place_windows(held_ref, wide_ref, places)
    finish(field_ref, gain_ref, wide_ref, out_ref, out_any, out_sems)
    each_block(lambda copy: copy.wait())


def backward_mix(delta, taps_spec, saved, gain, lengths, place, into, back, slices):
    rows, width = delta.shape
    size, reach = into.shape
    windows = lengths.shape[1]
    blocks = pltpu.HBM((slices // 2, reach // slices, width), jnp.bfloat16)
    return pl.pallas_call(
        backward_kernel,
        in_specs=[SCALARS, SCALARS, FAR, LOCAL] + [FAR] * 4,
        out_specs=[FAR] * 3,
        out_shape=[pltpu.HBM((rows, width), jnp.bfloat16), blocks, blocks],
        scratch_shapes=[
            pltpu.VMEM((rows, width), jnp.bfloat16),
            pltpu.VMEM((size, reach), jnp.bfloat16),
            pltpu.VMEM((reach, size), jnp.bfloat16),
            pltpu.VMEM((size, width), jnp.bfloat16),
            pltpu.VMEM((rows, width), jnp.bfloat16),
            pltpu.VMEM((size, windows * width), jnp.bfloat16),
            pltpu.VMEM((reach, width), jnp.bfloat16),
            pltpu.VMEM((reach, windows * width), jnp.bfloat16),
            pltpu.VMEM((size, (windows + 1) * width), jnp.bfloat16),
            pltpu.VMEM((windows, width // LANES, reach, LANES), jnp.float32),
            pltpu.VMEM((width // LANES, rows + reach // 2, LANES), jnp.float32),
            pltpu.SemaphoreType.DMA((2,)),
            pltpu.SemaphoreType.DMA((3, 4)),
            pltpu.SemaphoreType.DMA((slices,)),
            pltpu.SemaphoreType.DMA((4,)),
        ],
        compiler_params=params(40),
        cost_estimate=cost(7 * rows * size * width, 4 * rows * size + 16 * size * width),
        name="backward_mix",
    )(
        lengths, place, far(delta), gain, far(into), far(back), far(taps_spec), far(saved)
    )


def total_kernel(own_ref, *refs):
    total = own_ref[...]
    for come_ref in refs[:-1]:
        total = total + come_ref[...].astype(jnp.float32)
    refs[-1][...] = total * (1.0 / (2 * len(refs)))


def total_blocks(own, come):
    return pl.pallas_call(
        total_kernel,
        in_specs=[LOCAL] * (1 + len(come)),
        out_specs=LOCAL,
        out_shape=jax.ShapeDtypeStruct(own.shape, jnp.float32),
        compiler_params=params(4),
        name="total_blocks",
    )(own, *come)


def merge_kernel(kept_ref, come_ref, own_ref, *sent_refs):
    for slot in range(kept_ref.shape[0]):
        block = kept_ref[slot].astype(jnp.float32) + come_ref[slot].astype(jnp.float32)
        if slot == 0:
            own_ref[...] = block
        else:
            sent_refs[slot - 1][...] = block.astype(jnp.bfloat16)


def merge_blocks(kept, come):
    slots, height, width = kept.shape
    return pl.pallas_call(
        merge_kernel,
        in_specs=[LOCAL] * 2,
        out_specs=[LOCAL] * slots,
        out_shape=[jax.ShapeDtypeStruct((height, width), jnp.float32)]
        + [jax.ShapeDtypeStruct((height, width), jnp.bfloat16)] * (slots - 1),
        compiler_params=params(4),
        name="merge_blocks",
    )(kept, come)


def swap(pieces):
    return lax.all_to_all(pieces, "ctx", split_axis=0, concat_axis=0, tiled=True)


def from_core(away):
    count = lax.axis_size("dp")
    return lax.ppermute(away, "dp", [(i, i ^ 1) for i in range(count)])


def from_chips(blocks):
    count = lax.axis_size("dp")
    return [
        lax.ppermute(block, "dp", [(i, i ^ (2 * step)) for i in range(count)])
        for step, block in enumerate(blocks, 1)
    ]


def shards(queries, key_inputs, value_inputs, cotangent, filter_taps, skip_gain, lengths):
    groups = lax.axis_size("ctx")
    slices = lax.axis_size("dp")
    rows = queries.shape[1]
    total = rows * groups
    reach, width = filter_taps.shape
    into, back = transform_tables(reach)
    into, back = jnp.asarray(into), jnp.asarray(back)
    gain = skip_gain[None, :]
    place = lax.axis_index("dp").astype(jnp.int32).reshape(1)
    product = pair_product(key_inputs[0], value_inputs[0], groups)
    product_cols = swap(product)
    filter_taps, product = lax.optimization_barrier((filter_taps, product))
    taps_spec = taps_spectrum(filter_taps, into)
    delta = pair_product(cotangent[0], queries[0], groups)
    delta, taps_spec = lax.optimization_barrier((delta, taps_spec))
    delta_cols = swap(delta)
    mixing, saved = forward_mix(
        product_cols.reshape(total, width), taps_spec, gain, lengths, into, back
    )
    mixing_rows = swap(mixing.reshape(groups, rows, width))
    units, kept, away = backward_mix(
        delta_cols.reshape(total, width), taps_spec, saved, gain, lengths, place, into, back, slices
    )
    units_rows = swap(units.reshape(groups, rows, width))
    own, *sent = merge_blocks(kept, from_core(away))
    came = from_chips(sent)
    own, mixing_rows = lax.optimization_barrier((own, mixing_rows))
    mixed_out, query_grad, key_near = gate_both(
        mixing_rows, queries[0], cotangent[0], key_inputs[0]
    )
    *came, mixed_out = lax.optimization_barrier((*came, mixed_out))
    filter_grad = total_blocks(own, came)
    key_grad, value_grad = gate_last(units_rows, value_inputs[0], key_near)
    return (mixed_out[None], query_grad[None], key_grad[None], value_grad[None], filter_grad)


def solution(mesh):
    rows_spec = P("dp", "ctx", None)
    in_specs = (rows_spec,) * 4 + (P(None, "ctx"), P("ctx"), P("dp", None))
    out_specs = (rows_spec,) * 4 + (P("dp", "ctx"),)
    return jax.shard_map(shards, mesh=mesh, in_specs=in_specs, out_specs=out_specs, check_vma=False)
```

time: 507 us -> 91.7 us (0.18); the launches traced: 498 us -> 91 us
  matrix products: 153 us -> 0 us
  other arithmetic: 139 us -> 0 us
  local copies, waits for them, and re-layouts: 114 us -> 0.97 us
  Pallas kernels: 0 us -> 39.9 us
  blocking collectives: 18 us -> 0 us
  waiting for transfers between devices: 40.9 us -> 24.9 us
  between operations: 15.6 us -> 0.95 us
  starting transfers between devices: 17.1 us -> 24.3 us
    dot_general x28 -> x0, matrix products: 153 us -> none  [the longest x7 44.4 us: forward_dft(): jnp.einsum('rka,abc->rkbc', first, shaped, precision=lax.Precision.HIGHEST)]
    unnamed x4 -> x0, other arithmetic: 69 us -> none
    unnamed x111 -> x10, local copies, waits for them, and re-layouts: 41.2 us -> 0.97 us
    pallas_call x0 -> x9, Pallas kernels: none -> 39.9 us  [the longest x1 12.9 us: backward_mix(): pl.pallas_call(backward_kernel, in_specs=[SCALARS, SCALARS, FAR, LOCAL] +...]
    convert_element_type x2 -> x0, local copies, waits for them, and re-layouts: 33.7 us -> none  [the longest x1 17 us: shards(): delta = (cot_wide * query_wide).astype(jnp.bfloat16)]
    add x7 -> x0, other arithmetic: 29.9 us -> none  [the longest x5 21.5 us: times_conj(): left[0] * right[0] + left[1] * right[1]]
    broadcast_in_dim x2 -> x0, local copies, waits for them, and re-layouts: 23.5 us -> none  [the longest x1 11.7 us: shards(): units[None]]
    all_to_all x1 -> x0, blocking collectives: 18 us -> none  [shards(): lax.all_to_all(product, 'ctx', split_axis=2, concat_axis=1, tiled=True)]
  transfers between devices with their start and end apart: 4 -> 8, of which waited for: 4 -> 7; matrix products, arithmetic and copies ran while one was open for 7% -> 0% of each run, Pallas kernels for 0% -> 39%
where the time goes in v2:
time: 91.7 us; the launch traced here: 91 us
  Pallas kernels  39.9 us (44%)
  waiting for transfers between devices  24.9 us (27%)
  starting transfers between devices  24.3 us (26%)
  local copies, waits for them, and re-layouts  0.97 us (1%)
  between operations  0.95 us (1%)
    all_to_all x4, waiting for transfers between devices, swap(): lax.all_to_all(pieces, 'ctx', split_axis=0, concat_axis=0, tiled=True)  20.8 us
    all_to_all x4, starting transfers between devices, swap(): lax.all_to_all(pieces, 'ctx', split_axis=0, concat_axis=0, tiled=True)  19.4 us
    pallas_call x1, Pallas kernels, backward_mix(): pl.pallas_call(backward_kernel, in_specs=[SCALARS, SCALARS, FAR, LOCAL] +...  12.9 us
    pallas_call x1, Pallas kernels, forward_mix(): pl.pallas_call(forward_kernel, in_specs=[SCALARS, FAR, LOCAL, FAR, FAR, F...  10.8 us
    pallas_call x1, Pallas kernels, taps_spectrum(): pl.pallas_call(taps_kernel, in_specs=[FAR] * 2, out_specs=FAR, out_shape=...  5.59 us
    ppermute x3, starting transfers between devices, from_chips(): lax.ppermute(block, 'dp', [(i, i ^ 2 * step) for i in range(count)])  4.78 us
    pallas_call x2, Pallas kernels, pair_product(): pl.pallas_call(pair_kernel, in_specs=[FAR] * 2, out_specs=FAR, out_shape=...  4.77 us
    pallas_call x1, Pallas kernels, gate_both(): pl.pallas_call(gate_kernel, in_specs=[pl.BlockSpec(memory_space=pl.ANY)]...  2.6 us
  transfers between devices with their start and end apart: 8, of which 7 were waited for; matrix products, arithmetic and copies ran while one was open for 0% of the time, Pallas kernels for 39%

profile of v2, /device:TPU:0, one launch (start us, length us, event | category | flops | bytes accessed | tf_op | source)
XLA Modules:
  0.0 91.0 jit_solution(15036099320580207377)
XLA Ops:
  0.6 2.4 %pair_product.3 = bf16[16,128,256]{2,1,0:T(8,128)(2,1)} custom-call(bf16[128,4096]{1,0:T(8,128)(2,1)} %bitcast.18, bf16[128,4096]{1,0:T(8,128)(2,1)} %bitcast.16), custom_call_target="tpu_custom_call" | custom-call | flops 524288 | bytes 3145728 | tf_op jit(solution)/shard_map/pair_product/pallas_call | solution.py:79
  3.0 8.1 %all-to-all-start.1 = ((bf16[16,128,256]{2,1,0:T(8,128)(2,1)}), bf16[16,128,256]{2,1,0:T(8,128)(2,1)S(1)}, u32[]{:S(2)}, u32[]{:S(2)}) async-start(bf16[16,128,256]{2,1,0:T(8,128)(2,1)} %pair_product.3), calls=%async_computation.1 | async-start | bytes 2097152 | tf_op jit(solution)/shard_map/all_to_all | solution.py:618
  11.2 2.4 %pair_product.2 = bf16[16,128,256]{2,1,0:T(8,128)(2,1)} custom-call(bf16[128,4096]{1,0:T(8,128)(2,1)} %bitcast.22, bf16[128,4096]{1,0:T(8,128)(2,1)} %bitcast.20), custom_call_target="tpu_custom_call" | custom-call | flops 524288 | bytes 3145728 | tf_op jit(solution)/shard_map/pair_product/pallas_call | solution.py:79
  13.6 0.0 copy-start.1
  13.6 0.0 copy-start.2
  13.6 5.6 %taps_spectrum.1.taps_any = bf16[2048,256]{1,0:T(8,128)(2,1)} custom-call(f32[1024,256]{1,0:T(8,128)} %taps_any, bf16[2048,1024]{1,0:T(8,128)(2,1)} %constant.10.clone.into_any), custom_call_target="tpu_custom_call" | custom-call | flops 1073741824 | bytes 6291456 | tf_op jit(solution)/shard_map/taps_spectrum/pallas_call | solution.py:234
  19.2 9.6 %all-to-all-done.1 = bf16[16,128,256]{2,1,0:T(8,128)(2,1)S(1)} async-done(((bf16[16,128,256]{2,1,0:T(8,128)(2,1)}), bf16[16,128,256]{2,1,0:T(8,128)(2,1)S(1)}, u32[]{:S(2)}, u32[]{:S(2)}) %all-to-all-start.1) | async-done | bytes 1048608 | tf_op jit(solution)/shard_map/all_to_all | solution.py:618
  28.8 3.7 %all-to-all-start = ((bf16[16,128,256]{2,1,0:T(8,128)(2,1)}), bf16[16,128,256]{2,1,0:T(8,128)(2,1)S(1)}, u32[]{:S(2)}, u32[]{:S(2)}) async-start(bf16[16,128,256]{2,1,0:T(8,128)(2,1)} %pair_product.2), calls=%async_computation | async-start | bytes 2097152 | tf_op jit(solution)/shard_map/all_to_all | solution.py:618
  32.5 0.0 copy-done.4
  32.5 0.0 copy-done.1
  32.5 0.0 copy-done.2
  32.5 10.8 %forward_mix.1 = (bf16[2048,256]{1,0:T(8,128)(2,1)}, bf16[2048,768]{1,0:T(8,128)(2,1)}) custom-call(s32[1,3]{1,0:T(1,128)S(1)} %copy-done.2, bf16[2048,256]{1,0:T(8,128)(2,1)} %bitcast.27, f32[1,256]{1,0:T(1,128)S(1)} %bitcast.14, bf16[2048,1024]{1,0:T(8,128)(2,1)} %constant.10.clone.into_any, bf16[1024,2048]{1,0:T(8,128)(2,1)} %constant.11.clone.back_any, ...), custom_call_target="tpu_custom_call" | custom-call | flops 6442450944 | bytes 25165824 | tf_op jit(solution)/shard_map/forward_mix/pallas_call | solution.py:426
  43.4 5.4 %all-to-all-done = bf16[16,128,256]{2,1,0:T(8,128)(2,1)S(1)} async-done(((bf16[16,128,256]{2,1,0:T(8,128)(2,1)}), bf16[16,128,256]{2,1,0:T(8,128)(2,1)S(1)}, u32[]{:S(2)}, u32[]{:S(2)}) %all-to-all-start) | async-done | bytes 1048608 | tf_op jit(solution)/shard_map/all_to_all | solution.py:618
  48.8 3.8 %all-to-all-start.2 = ((bf16[16,128,256]{2,1,0:T(8,128)(2,1)}), bf16[16,128,256]{2,1,0:T(8,128)(2,1)S(1)}, u32[]{:S(2)}, u32[]{:S(2)}) async-start(bf16[16,128,256]{2,1,0:T(8,128)(2,1)} %bitcast.26), calls=%async_computation.2 | async-start | bytes 2097152 | tf_op jit(solution)/shard_map/all_to_all | solution.py:618
  52.7 0.0 copy-done.3
  52.7 12.9 %backward_mix.1 = (bf16[2048,256]{1,0:T(8,128)(2,1)}, bf16[4,128,256]{2,1,0:T(8,128)(2,1)}, bf16[4,128,256]{2,1,0:T(8,128)(2,1)}) custom-call(s32[1,3]{1,0:T(1,128)S(1)} %copy-done.2, s32[1]{0:T(128)} %bitcast.place_ref, bf16[2048,256]{1,0:T(8,128)(2,1)} %bitcast.25, f32[1,256]{1,0:T(1,128)S(1)} %bitcast.15, bf16[2048,1024]{1,0:T(8,128)(2,1)} %constant.10.clone.into_any, ...), custom_call_target="tpu_custom_call" | custom-call | flops 7516192768 | bytes 25165824 | tf_op jit(solution)/shard_map/backward_mix/pallas_call | solution.py:547
  65.6 3.2 %all-to-all-done.2.inner_any = bf16[16,128,256]{2,1,0:T(8,128)(2,1)S(1)} async-done(((bf16[16,128,256]{2,1,0:T(8,128)(2,1)}), bf16[16,128,256]{2,1,0:T(8,128)(2,1)S(1)}, u32[]{:S(2)}, u32[]{:S(2)}) %all-to-all-start.2) | async-done | bytes 1048608 | tf_op jit(solution)/shard_map/all_to_all | solution.py:618
  68.8 3.8 %all-to-all-start.3 = ((bf16[16,128,256]{2,1,0:T(8,128)(2,1)}), bf16[16,128,256]{2,1,0:T(8,128)(2,1)S(1)}, u32[]{:S(2)}, u32[]{:S(2)}) async-start(bf16[16,128,256]{2,1,0:T(8,128)(2,1)} %bitcast.24), calls=%async_computation.3 | async-start | bytes 2097152 | tf_op jit(solution)/shard_map/all_to_all | solution.py:618
  72.6 0.1 collective-permute-start
  72.7 1.7 %collective-permute-done.come_ref = bf16[4,128,256]{2,1,0:T(8,128)(2,1)S(1)} collective-permute-done((bf16[4,128,256]{2,1,0:T(8,128)(2,1)}, bf16[4,128,256]{2,1,0:T(8,128)(2,1)S(1)}, u32[]{:S(2)}, u32[]{:S(2)}) %collective-permute-start) | collective-permute-done | bytes 262176 | tf_op jit(solution)/shard_map/ppermute | solution.py:623
  74.4 0.9 %copy-done = bf16[4,128,256]{2,1,0:T(8,128)(2,1)S(1)} copy-done((bf16[4,128,256]{2,1,0:T(8,128)(2,1)S(1)}, bf16[4,128,256]{2,1,0:T(8,128)(2,1)}, u32[]{:S(2)}) %copy-start) | copy-done | bytes 262168
  75.3 0.1 merge_blocks.1
  75.4 1.6 %collective-permute-start.1 = (bf16[128,256]{1,0:T(8,128)(2,1)S(1)}, bf16[128,256]{1,0:T(8,128)(2,1)S(1)}, u32[]{:S(2)}, u32[]{:S(2)}) collective-permute-start(bf16[128,256]{1,0:T(8,128)(2,1)S(1)} %get-tuple-element.34), channel_id=1, source_target_pairs={{0,32},{16,48},{32,0},{48,16},{64,96},{80,112},{96,64},{112,80},{1... | collective-permute-start | bytes 196616 | tf_op jit(solution)/shard_map/ppermute | solution.py:629
  77.0 2.7 %collective-permute-start.2 = (bf16[128,256]{1,0:T(8,128)(2,1)S(1)}, bf16[128,256]{1,0:T(8,128)(2,1)S(1)}, u32[]{:S(2)}, u32[]{:S(2)}) collective-permute-start(bf16[128,256]{1,0:T(8,128)(2,1)S(1)} %get-tuple-element.35), channel_id=1, source_target_pairs={{0,64},{16,80},{32,96},{48,112},{64,0},{80,16},{96,32},{112,48},{1... | collective-permute-start | bytes 196616 | tf_op jit(solution)/shard_map/ppermute | solution.py:629
  79.7 0.5 collective-permute-start.3
  80.2 2.6 %gate_both.1 = (bf16[128,4096]{1,0:T(8,128)(2,1)}, bf16[128,4096]{1,0:T(8,128)(2,1)}, bf16[128,4096]{1,0:T(8,128)(2,1)S(1)}) custom-call(bf16[16,128,256]{2,1,0:T(8,128)(2,1)S(1)} %all-to-all-done.2.inner_any, bf16[128,4096]{1,0:T(8,128)(2,1)} %bitcast.21, bf16[128,4096]{1,0:T(8,128)(2,1)} %bitcast.23, bf16[128,4096]{1,0:T(8,128)(2,1)} %bitcast.19), custom_call_target="tpu_custom_call" | custom-call | flops 1048576 | bytes 6291456 | tf_op jit(solution)/shard_map/gate_both/pallas_call | solution.py:142
  82.8 0.0 collective-permute-done.1.refs_0_
  82.8 0.4 collective-permute-done.2.refs_1_
  83.2 2.0 %collective-permute-done.3.refs_2_ = bf16[128,256]{1,0:T(8,128)(2,1)S(1)} collective-permute-done((bf16[128,256]{1,0:T(8,128)(2,1)S(1)}, bf16[128,256]{1,0:T(8,128)(2,1)S(1)}, u32[]{:S(2)}, u32[]{:S(2)}) %collective-permute-start.3) | collective-permute-done | bytes 65568 | tf_op jit(solution)/shard_map/ppermute | solution.py:629
  85.2 0.7 total_blocks.1
  85.9 2.5 %all-to-all-done.3.inner_ref = bf16[16,128,256]{2,1,0:T(8,128)(2,1)S(1)} async-done(((bf16[16,128,256]{2,1,0:T(8,128)(2,1)}), bf16[16,128,256]{2,1,0:T(8,128)(2,1)S(1)}, u32[]{:S(2)}, u32[]{:S(2)}) %all-to-all-start.3) | async-done | bytes 1048608 | tf_op jit(solution)/shard_map/all_to_all | solution.py:618
  88.4 2.4 %gate_last.1 = (bf16[128,4096]{1,0:T(8,128)(2,1)}, bf16[128,4096]{1,0:T(8,128)(2,1)}) custom-call(bf16[16,128,256]{2,1,0:T(8,128)(2,1)S(1)} %all-to-all-done.3.inner_ref, bf16[128,4096]{1,0:T(8,128)(2,1)} %bitcast.17, bf16[128,4096]{1,0:T(8,128)(2,1)S(1)} %get-tuple-element.44.second_ref), custom_call_target="tpu_custom_call" | custom-call | flops 1048576 | bytes 5242880 | tf_op jit(solution)/shard_map/gate_last/pallas_call | solution.py:193
  (3 shorter events, 0.0 us)
Async XLA Ops:
  3.0 25.8 %all-to-all-start.1 = ((bf16[16,128,256]{2,1,0:T(8,128)(2,1)}), bf16[16,128,256]{2,1,0:T(8,128)(2,1)S(1)}, u32[]{:S(2)}, u32[]{:S(2)}) async-start(bf16[16,128,256]{2,1,0:T(8,128)(2,1)} %pair_product.3), calls=%async_computation.1 | async-start | bytes 2097152 | tf_op jit(solution)/shard_map/all_to_all | solution.py:618
  13.6 18.9 %copy-start.1 = (f32[256]{0:T(256)S(1)}, f32[256]{0:T(256)}, u32[]{:S(2)}) copy-start(f32[256]{0:T(256)} %param.14) | copy-start | bytes 3076
  13.6 18.9 %copy-start.2 = (s32[1,3]{1,0:T(1,128)S(1)}, s32[1,3]{1,0:T(1,128)}, u32[]{:S(2)}) copy-start(s32[1,3]{1,0:T(1,128)} %lengths_ref.3) | copy-start | bytes 40
  28.8 3.7 %copy-start.4 = (bf16[16,128,256]{2,1,0:T(8,128)(2,1)}, bf16[16,128,256]{2,1,0:T(8,128)(2,1)S(1)}, u32[]{:S(2)}) copy-start(bf16[16,128,256]{2,1,0:T(8,128)(2,1)S(1)} %all-to-all-done.1) | copy-start | bytes 3145732
  28.8 20.0 %all-to-all-start = ((bf16[16,128,256]{2,1,0:T(8,128)(2,1)}), bf16[16,128,256]{2,1,0:T(8,128)(2,1)S(1)}, u32[]{:S(2)}, u32[]{:S(2)}) async-start(bf16[16,128,256]{2,1,0:T(8,128)(2,1)} %pair_product.2), calls=%async_computation | async-start | bytes 2097152 | tf_op jit(solution)/shard_map/all_to_all | solution.py:618
  48.8 3.9 %copy-start.3 = (bf16[16,128,256]{2,1,0:T(8,128)(2,1)}, bf16[16,128,256]{2,1,0:T(8,128)(2,1)S(1)}, u32[]{:S(2)}) copy-start(bf16[16,128,256]{2,1,0:T(8,128)(2,1)S(1)} %all-to-all-done) | copy-start | bytes 3145732
  48.8 19.9 %all-to-all-start.2 = ((bf16[16,128,256]{2,1,0:T(8,128)(2,1)}), bf16[16,128,256]{2,1,0:T(8,128)(2,1)S(1)}, u32[]{:S(2)}, u32[]{:S(2)}) async-start(bf16[16,128,256]{2,1,0:T(8,128)(2,1)} %bitcast.26), calls=%async_computation.2 | async-start | bytes 2097152 | tf_op jit(solution)/shard_map/all_to_all | solution.py:618
  68.8 19.7 %all-to-all-start.3 = ((bf16[16,128,256]{2,1,0:T(8,128)(2,1)}), bf16[16,128,256]{2,1,0:T(8,128)(2,1)S(1)}, u32[]{:S(2)}, u32[]{:S(2)}) async-start(bf16[16,128,256]{2,1,0:T(8,128)(2,1)} %bitcast.24), calls=%async_computation.3 | async-start | bytes 2097152 | tf_op jit(solution)/shard_map/all_to_all | solution.py:618
  72.6 1.8 %collective-permute-start = (bf16[4,128,256]{2,1,0:T(8,128)(2,1)}, bf16[4,128,256]{2,1,0:T(8,128)(2,1)S(1)}, u32[]{:S(2)}, u32[]{:S(2)}) collective-permute-start(bf16[4,128,256]{2,1,0:T(8,128)(2,1)} %get-tuple-element.33), channel_id=1, source_target_pairs={{0,16},{16,0},{32,48},{48,32},{64,80},{80,64},{96,112},{112,96},{1... | collective-permute-start | bytes 786440 | tf_op jit(solution)/shard_map/ppermute | solution.py:623
  74.4 1.0 %copy-start = (bf16[4,128,256]{2,1,0:T(8,128)(2,1)S(1)}, bf16[4,128,256]{2,1,0:T(8,128)(2,1)}, u32[]{:S(2)}) copy-start(bf16[4,128,256]{2,1,0:T(8,128)(2,1)} %get-tuple-element.32.kept_ref) | copy-start | bytes 786436
  75.4 7.4 %collective-permute-start.1 = (bf16[128,256]{1,0:T(8,128)(2,1)S(1)}, bf16[128,256]{1,0:T(8,128)(2,1)S(1)}, u32[]{:S(2)}, u32[]{:S(2)}) collective-permute-start(bf16[128,256]{1,0:T(8,128)(2,1)S(1)} %get-tuple-element.34), channel_id=1, source_target_pairs={{0,32},{16,48},{32,0},{48,16},{64,96},{80,112},{96,64},{112,80},{1... | collective-permute-start | bytes 196616 | tf_op jit(solution)/shard_map/ppermute | solution.py:629
  77.0 6.3 %collective-permute-start.2 = (bf16[128,256]{1,0:T(8,128)(2,1)S(1)}, bf16[128,256]{1,0:T(8,128)(2,1)S(1)}, u32[]{:S(2)}, u32[]{:S(2)}) collective-permute-start(bf16[128,256]{1,0:T(8,128)(2,1)S(1)} %get-tuple-element.35), channel_id=1, source_target_pairs={{0,64},{16,80},{32,96},{48,112},{64,0},{80,16},{96,32},{112,48},{1... | collective-permute-start | bytes 196616 | tf_op jit(solution)/shard_map/ppermute | solution.py:629
  79.7 5.5 %collective-permute-start.3 = (bf16[128,256]{1,0:T(8,128)(2,1)S(1)}, bf16[128,256]{1,0:T(8,128)(2,1)S(1)}, u32[]{:S(2)}, u32[]{:S(2)}) collective-permute-start(bf16[128,256]{1,0:T(8,128)(2,1)S(1)} %get-tuple-element.36), channel_id=1, source_target_pairs={{0,96},{16,112},{32,64},{48,80},{64,32},{80,48},{96,0},{112,16},{1... | collective-permute-start | bytes 196616 | tf_op jit(solution)/shard_map/ppermute | solution.py:629

commit v3 on v2

--- a/solution.py
+++ b/solution.py
@@ -71,26 +71,6 @@
         stores.append(copy)
     for copy in stores:
         copy.wait()
-
-
-def pair_product(left, right, groups):
-    rows, columns = left.shape
-    shape = (groups, rows, columns // groups)
-    return pl.pallas_call(
-        pair_kernel,
-        in_specs=[FAR] * 2,
-        out_specs=FAR,
-        out_shape=pltpu.HBM(shape, jnp.bfloat16),
-        scratch_shapes=[
-            pltpu.VMEM((rows, columns), jnp.bfloat16),
-            pltpu.VMEM((rows, columns), jnp.bfloat16),
-            pltpu.VMEM(shape, jnp.bfloat16),
-            pltpu.SemaphoreType.DMA((3, 4)),
-        ],
-        compiler_params=params(8),
-        cost_estimate=cost(rows * columns, 6 * rows * columns),
-        name="pair_product",
-    )(far(left), far(right))
 
 
 def gate_kernel(
@@ -228,24 +208,78 @@
         copy.wait()
 
 
-def taps_spectrum(taps, into):
+def opening_kernel(
+    key_any, value_any, cot_any, query_any, taps_any, into_any,
+    product_any, delta_any, spectrum_any,
+    left_ref, right_ref, pair_ref, pair_sems, taps_ref, into_ref, spectrum_ref, taps_sems,
+):
+    pair = (left_ref, right_ref, pair_ref, pair_sems)
+    pair_kernel(key_any, value_any, product_any, *pair)
+
+    @pl.when(lax.axis_index("dp") % 2 == 1)
+    def _():
+        pair_kernel(cot_any, query_any, delta_any, *pair)
+        taps_kernel(taps_any, into_any, spectrum_any, taps_ref, into_ref, spectrum_ref, taps_sems)
+
+
+def second_kernel(
+    cot_any, query_any, taps_any, into_any, _, __, delta_any, spectrum_any,
+    left_ref, right_ref, pair_ref, pair_sems, taps_ref, into_ref, spectrum_ref, taps_sems,
+):
+    @pl.when(lax.axis_index("dp") % 2 == 0)
+    def _():
+        pair_kernel(
+            cot_any, query_any, delta_any, left_ref, right_ref, pair_ref, pair_sems
+        )
+        taps_kernel(taps_any, into_any, spectrum_any, taps_ref, into_ref, spectrum_ref, taps_sems)
+
+
+def opening_scratch(rows, columns, groups, reach, size, width):
+    return [
+        pltpu.VMEM((rows, columns), jnp.bfloat16),
+        pltpu.VMEM((rows, columns), jnp.bfloat16),
+        pltpu.VMEM((groups, rows, columns // groups), jnp.bfloat16),
+        pltpu.SemaphoreType.DMA((3, 4)),
+        pltpu.VMEM((reach, width), jnp.float32),
+        pltpu.VMEM((size, reach), jnp.bfloat16),
+        pltpu.VMEM((size, width), jnp.bfloat16),
+        pltpu.SemaphoreType.DMA((3, size // TILE)),
+    ]
+
+
+def opening(key, value, cotangent, queries, taps, into, groups):
+    rows, columns = key.shape
     reach, width = taps.shape
     size = into.shape[0]
-    return pl.pallas_call(
-        taps_kernel,
-        in_specs=[FAR] * 2,
-        out_specs=FAR,
-        out_shape=pltpu.HBM((size, width), jnp.bfloat16),
-        scratch_shapes=[
-            pltpu.VMEM((reach, width), jnp.float32),
-            pltpu.VMEM((size, reach), jnp.bfloat16),
-            pltpu.VMEM((size, width), jnp.bfloat16),
-            pltpu.SemaphoreType.DMA((3, size // TILE)),
-        ],
-        compiler_params=params(12),
+    pieces = pltpu.HBM((groups, rows, columns // groups), jnp.bfloat16)
+    return pl.pallas_call(
+        opening_kernel,
+        in_specs=[FAR] * 6,
+        out_specs=[FAR] * 3,
+        out_shape=[pieces, pieces, pltpu.HBM((size, width), jnp.bfloat16)],
+        scratch_shapes=opening_scratch(rows, columns, groups, reach, size, width),
+        compiler_params=params(20),
+        cost_estimate=cost(rows * columns, 6 * rows * columns),
+        name="opening",
+    )(far(key), far(value), far(cotangent), far(queries), far(taps), far(into))
+
+
+def second(cotangent, queries, taps, into, delta, spectrum):
+    rows, columns = queries.shape
+    reach, width = taps.shape
+    size = into.shape[0]
+    groups = delta.shape[0]
+    return pl.pallas_call(
+        second_kernel,
+        in_specs=[FAR] * 6,
+        out_specs=[FAR] * 2,
+        out_shape=[pltpu.HBM(delta.shape, delta.dtype), pltpu.HBM(spectrum.shape, spectrum.dtype)],
+        input_output_aliases={4: 0, 5: 1},
+        scratch_shapes=opening_scratch(rows, columns, groups, reach, size, width),
+        compiler_params=params(20),
         cost_estimate=cost(2 * reach * size * width, 2 * reach * size + 4 * size * width),
-        name="taps_spectrum",
-    )(far(taps), far(into))
+        name="second",
+    )(far(cotangent), far(queries), far(taps), far(into), far(delta), far(spectrum))
 
 
 def window_order(lengths_ref):
@@ -274,11 +308,14 @@
     return slots, places
 
 
-def spread(field_ref, wide_ref):
-    rows = field_ref.shape[0]
-    for half in range(wide_ref.shape[0]):
-        lanes = slice(half * LANES, (half + 1) * LANES)
-        wide_ref[half, :rows] = field_ref[:, lanes].astype(jnp.float32)
+def spread(field_ref, wide_ref, copies):
+    step = field_ref.shape[0] // len(copies)
+    for part, copy in enumerate(copies):
+        rows = slice(part * step, (part + 1) * step)
+        copy.wait()
+        for half in range(wide_ref.shape[0]):
+            lanes = slice(half * LANES, (half + 1) * LANES)
+            wide_ref[half, rows] = field_ref[rows, lanes].astype(jnp.float32)
 
 
 def take_windows(wide_ref, part_ref, slots):
@@ -288,7 +325,9 @@
         inside = lax.broadcasted_iota(jnp.int32, (rows, LANES), 0) < length
         for half in range(wide_ref.shape[0]):
             lane = (slot * wide_ref.shape[0] + half) * LANES
-            part = jnp.where(inside, wide_ref[half, pl.ds(start, rows)], 0.0)
+            part = wide_ref[half, pl.ds(start, rows)]
+            if slot > 0:
+                part = jnp.where(inside, part, 0.0)
             part_ref[:rows, lane : lane + LANES] = part.astype(jnp.bfloat16)
 
 
@@ -368,22 +407,21 @@
 def forward_kernel(
     lengths_ref, field_any, gain_ref, into_any, back_any, taps_any, out_any, saved_any,
     field_ref, into_ref, back_ref, taps_ref, out_ref, saved_ref,
-    part_ref, spectra_ref, held_ref, wide_ref, sems, load_sems, out_sems,
+    part_ref, spectra_ref, held_ref, wide_ref, field_sems, back_sem, load_sems, out_sems,
 ):
     size, reach = into_ref.shape
     width = taps_ref.shape[1]
     parts = load_sems.shape[1]
-    field_copy = pltpu.make_async_copy(field_any, field_ref, sems.at[0])
-    back_copy = pltpu.make_async_copy(back_any, back_ref, sems.at[1])
+    field_copies = copy_parts(field_any, field_ref, field_sems)
+    back_copy = pltpu.make_async_copy(back_any, back_ref, back_sem)
     into_copies = copy_parts(into_any, into_ref, load_sems.at[0])
     taps_copies = copy_parts(taps_any, taps_ref, load_sems.at[1])
     saved_copies = copy_parts(saved_ref, saved_any, load_sems.at[2])
     stages = [list(copies) for copies in zip(into_copies, taps_copies)]
-    begin([field_copy] + stages[0])
+    begin(field_copies + stages[0])
     slots, places = window_order(lengths_ref)
-    field_copy.wait()
+    spread(field_ref, wide_ref, field_copies)
     begin(stages[1] + stages[2])
-    spread(field_ref, wide_ref)
     take_windows(wide_ref, part_ref, slots)
     for low in range(0, size, TILE):
         part, start = divmod(low * parts, size)
@@ -442,7 +480,8 @@
             pltpu.VMEM((size, windows * width), jnp.bfloat16),
             pltpu.VMEM((windows, width // LANES, reach, LANES), jnp.float32),
             pltpu.VMEM((width // LANES, rows + reach // 2, LANES), jnp.float32),
-            pltpu.SemaphoreType.DMA((2,)),
+            pltpu.SemaphoreType.DMA((4,)),
+            pltpu.SemaphoreType.DMA,
             pltpu.SemaphoreType.DMA((3, 4)),
             pltpu.SemaphoreType.DMA((4,)),
         ],
@@ -453,25 +492,24 @@
 
 
 def backward_kernel(
-    lengths_ref, place_ref, field_any, gain_ref, into_any, back_any, taps_any, saved_any,
-    out_any, kept_any, away_any,
+    lengths_ref, field_any, gain_ref, into_any, back_any, taps_any, saved_any,
+    out_any, own_any, one_any, two_any, three_any,
     field_ref, into_ref, back_ref, taps_ref, out_ref, saved_ref, filter_ref,
-    part_ref, spectra_ref, held_ref, wide_ref, sems, load_sems, filter_sems, out_sems,
+    part_ref, spectra_ref, held_ref, wide_ref, field_sems, back_sem, load_sems, filter_sems, out_sems,
 ):
     size, reach = into_ref.shape
     width = taps_ref.shape[1]
     parts = load_sems.shape[1]
-    field_copy = pltpu.make_async_copy(field_any, field_ref, sems.at[0])
-    back_copy = pltpu.make_async_copy(back_any, back_ref, sems.at[1])
+    field_copies = copy_parts(field_any, field_ref, field_sems)
+    back_copy = pltpu.make_async_copy(back_any, back_ref, back_sem)
     into_copies = copy_parts(into_any, into_ref, load_sems.at[0])
     taps_copies = copy_parts(taps_any, taps_ref, load_sems.at[1])
     saved_copies = copy_parts(saved_any, saved_ref, load_sems.at[2])
     stages = [list(copies) for copies in zip(into_copies, taps_copies, saved_copies)]
-    begin([field_copy] + stages[0])
+    begin(field_copies + stages[0])
     slots, places = window_order(lengths_ref)
-    field_copy.wait()
+    spread(field_ref, wide_ref, field_copies)
     begin(stages[1] + stages[2])
-    spread(field_ref, wide_ref)
     take_windows(wide_ref, part_ref, slots)
     for low in range(0, size, TILE):
         part, start = divmod(low * parts, size)
@@ -508,21 +546,19 @@
             )
         filter_ref[rows] = terms.astype(jnp.bfloat16)
 
-    count, height, _ = kept_any.shape
-    core, chip = place_ref[0] % 2, place_ref[0] // 2
+    targets = (own_any, one_any, two_any, three_any)
+    height = own_any.shape[0]
+    chip = lax.axis_index("dp") // 2
 
     def each_block(act):
-        for block in range(2 * count):
+        for block in range(len(targets)):
             rows = pl.ds(block * height, height)
-            for same, target in ((0, kept_any), (1, away_any)):
-
-                @pl.when((core + block) % 2 == same)
+            for slot, target in enumerate(targets):
+
+                @pl.when((chip ^ block) == slot)
                 def _():
                     act(
-                        pltpu.make_async_copy(
-                            filter_ref.at[rows], target.at[(block // 2) ^ chip],
-                            filter_sems.at[block],
-                        )
+                        pltpu.make_async_copy(filter_ref.at[rows], target, filter_sems.at[block])
                     )
 
     each_block(lambda copy: copy.start())
@@ -539,16 +575,17 @@
     each_block(lambda copy: copy.wait())
 
 
-def backward_mix(delta, taps_spec, saved, gain, lengths, place, into, back, slices):
+def backward_mix(delta, taps_spec, saved, gain, lengths, into, back, slices):
     rows, width = delta.shape
     size, reach = into.shape
     windows = lengths.shape[1]
-    blocks = pltpu.HBM((slices // 2, reach // slices, width), jnp.bfloat16)
+    chips = slices // 2
+    block = pltpu.HBM((reach // chips, width), jnp.bfloat16)
     return pl.pallas_call(
         backward_kernel,
-        in_specs=[SCALARS, SCALARS, FAR, LOCAL] + [FAR] * 4,
-        out_specs=[FAR] * 3,
-        out_shape=[pltpu.HBM((rows, width), jnp.bfloat16), blocks, blocks],
+        in_specs=[SCALARS, FAR, LOCAL] + [FAR] * 4,
+        out_specs=[FAR] * (1 + chips),
+        out_shape=[pltpu.HBM((rows, width), jnp.bfloat16)] + [block] * chips,
         scratch_shapes=[
             pltpu.VMEM((rows, width), jnp.bfloat16),
             pltpu.VMEM((size, reach), jnp.bfloat16),
@@ -561,16 +598,17 @@
             pltpu.VMEM((size, (windows + 1) * width), jnp.bfloat16),
             pltpu.VMEM((windows, width // LANES, reach, LANES), jnp.float32),
             pltpu.VMEM((width // LANES, rows + reach // 2, LANES), jnp.float32),
-            pltpu.SemaphoreType.DMA((2,)),
+            pltpu.SemaphoreType.DMA((4,)),
+            pltpu.SemaphoreType.DMA,
             pltpu.SemaphoreType.DMA((3, 4)),
-            pltpu.SemaphoreType.DMA((slices,)),
+            pltpu.SemaphoreType.DMA((chips,)),
             pltpu.SemaphoreType.DMA((4,)),
         ],
         compiler_params=params(40),
         cost_estimate=cost(7 * rows * size * width, 4 * rows * size + 16 * size * width),
         name="backward_mix",
     )(
-        lengths, place, far(delta), gain, far(into), far(back), far(taps_spec), far(saved)
+        lengths, far(delta), gain, far(into), far(back), far(taps_spec), far(saved)
     )
 
 
@@ -592,25 +630,44 @@
     )(own, *come)
 
 
-def merge_kernel(kept_ref, come_ref, own_ref, *sent_refs):
-    for slot in range(kept_ref.shape[0]):
-        block = kept_ref[slot].astype(jnp.float32) + come_ref[slot].astype(jnp.float32)
-        if slot == 0:
-            own_ref[...] = block
-        else:
-            sent_refs[slot - 1][...] = block.astype(jnp.bfloat16)
-
-
-def merge_blocks(kept, come):
-    slots, height, width = kept.shape
+def merge_kernel(own_ref, one_ref, two_ref, three_ref, kept_ref, away_ref, held_ref):
+    terms = [ref[...].astype(jnp.float32) for ref in (own_ref, one_ref, two_ref, three_ref)]
+    held_ref[...] = (terms[0] + terms[1]) + (terms[2] + terms[3])
+    height = kept_ref.shape[0]
+    core = lax.axis_index("dp") % 2
+    kept_ref[...] = held_ref[pl.ds(pl.multiple_of(core * height, height), height)]
+    away = held_ref[pl.ds(pl.multiple_of((1 - core) * height, height), height)]
+    away_ref[...] = away.astype(jnp.bfloat16)
+
+
+def merge_blocks(own, came):
+    height, width = own.shape
     return pl.pallas_call(
         merge_kernel,
-        in_specs=[LOCAL] * 2,
-        out_specs=[LOCAL] * slots,
-        out_shape=[jax.ShapeDtypeStruct((height, width), jnp.float32)]
-        + [jax.ShapeDtypeStruct((height, width), jnp.bfloat16)] * (slots - 1),
+        in_specs=[LOCAL] * (1 + len(came)),
+        out_specs=[LOCAL] * 2,
+        out_shape=[
+            jax.ShapeDtypeStruct((height // 2, width), jnp.float32),
+            jax.ShapeDtypeStruct((height // 2, width), jnp.bfloat16),
+        ],
+        scratch_shapes=[pltpu.VMEM((height, width), jnp.float32)],
         compiler_params=params(4),
         name="merge_blocks",
+    )(own, *came)
+
+
+def total_kernel(kept_ref, come_ref, out_ref):
+    out_ref[...] = (kept_ref[...] + come_ref[...].astype(jnp.float32)) * (1.0 / 8)
+
+
+def total_blocks(kept, come):
+    return pl.pallas_call(
+        total_kernel,
+        in_specs=[LOCAL] * 2,
+        out_specs=LOCAL,
+        out_shape=jax.ShapeDtypeStruct(kept.shape, jnp.float32),
+        compiler_params=params(4),
+        name="total_blocks",
     )(kept, come)
 
 
@@ -640,30 +697,28 @@
     into, back = transform_tables(reach)
     into, back = jnp.asarray(into), jnp.asarray(back)
     gain = skip_gain[None, :]
-    place = lax.axis_index("dp").astype(jnp.int32).reshape(1)
-    product = pair_product(key_inputs[0], value_inputs[0], groups)
+    product, delta, taps_spec = opening(
+        key_inputs[0], value_inputs[0], cotangent[0], queries[0], filter_taps, into, groups
+    )
     product_cols = swap(product)
-    filter_taps, product = lax.optimization_barrier((filter_taps, product))
-    taps_spec = taps_spectrum(filter_taps, into)
-    delta = pair_product(cotangent[0], queries[0], groups)
-    delta, taps_spec = lax.optimization_barrier((delta, taps_spec))
+    delta, taps_spec = second(cotangent[0], queries[0], filter_taps, into, delta, taps_spec)
     delta_cols = swap(delta)
     mixing, saved = forward_mix(
         product_cols.reshape(total, width), taps_spec, gain, lengths, into, back
     )
     mixing_rows = swap(mixing.reshape(groups, rows, width))
-    units, kept, away = backward_mix(
-        delta_cols.reshape(total, width), taps_spec, saved, gain, lengths, place, into, back, slices
+    units, own, *blocks = backward_mix(
+        delta_cols.reshape(total, width), taps_spec, saved, gain, lengths, into, back, slices
     )
     units_rows = swap(units.reshape(groups, rows, width))
-    own, *sent = merge_blocks(kept, from_core(away))
-    came = from_chips(sent)
-    own, mixing_rows = lax.optimization_barrier((own, mixing_rows))
+    came = from_chips(blocks)
     mixed_out, query_grad, key_near = gate_both(
         mixing_rows, queries[0], cotangent[0], key_inputs[0]
     )
     *came, mixed_out = lax.optimization_barrier((*came, mixed_out))
-    filter_grad = total_blocks(own, came)
+    kept, away = merge_blocks(own, came)
+    filter_grad = total_blocks(kept, from_core(away))
+    units_rows, filter_grad = lax.optimization_barrier((units_rows, filter_grad))
     key_grad, value_grad = gate_last(units_rows, value_inputs[0], key_near)
     return (mixed_out[None], query_grad[None], key_grad[None], value_grad[None], filter_grad)
 

time: 91.7 us -> 89.8 us (0.979)
  the two profiles are of different devices: /device:TPU:0 before, /device:TPU:1 now
where the time goes in v3:
time: 89.8 us; the launch traced here: 89.2 us
  Pallas kernels  39.7 us (44%)
  starting transfers between devices  25.7 us (29%)
  waiting for transfers between devices  22.8 us (25%)
  between operations  0.94 us (1%)
    all_to_all x4, starting transfers between devices, swap(): lax.all_to_all(pieces, 'ctx', split_axis=0, concat_axis=0, tiled=True)  21.7 us
    all_to_all x4, waiting for transfers between devices, swap(): lax.all_to_all(pieces, 'ctx', split_axis=0, concat_axis=0, tiled=True)  18.7 us
    pallas_call x1, Pallas kernels, backward_mix(): pl.pallas_call(backward_kernel, in_specs=[SCALARS, FAR, LOCAL] + [FAR] *...  12.6 us
    pallas_call x1, Pallas kernels, forward_mix(): pl.pallas_call(forward_kernel, in_specs=[SCALARS, FAR, LOCAL, FAR, FAR, F...  10.7 us
    pallas_call x1, Pallas kernels, opening(): pl.pallas_call(opening_kernel, in_specs=[FAR] * 6, out_specs=[FAR] * 3, o...  10.2 us
    ppermute x3, starting transfers between devices, from_chips(): lax.ppermute(block, 'dp', [(i, i ^ 2 * step) for i in range(count)])  3.94 us
    ppermute x3, waiting for transfers between devices, from_chips(): lax.ppermute(block, 'dp', [(i, i ^ 2 * step) for i in range(count)])  2.89 us
    pallas_call x1, Pallas kernels, gate_both(): pl.pallas_call(gate_kernel, in_specs=[pl.BlockSpec(memory_space=pl.ANY)]...  2.6 us
  transfers between devices with their start and end apart: 8, of which 7 were waited for; matrix products, arithmetic and copies ran while one was open for 0% of the time, Pallas kernels for 30%

profile of v3, /device:TPU:1, one launch (start us, length us, event | category | flops | bytes accessed | tf_op | source)
XLA Modules:
  0.0 89.2 jit_solution(6218148211928154468)
XLA Ops:
  0.6 10.2 %opening.1 = (bf16[16,128,256]{2,1,0:T(8,128)(2,1)}, bf16[16,128,256]{2,1,0:T(8,128)(2,1)}, bf16[2048,256]{1,0:T(8,128)(2,1)}) custom-call(bf16[128,4096]{1,0:T(8,128)(2,1)} %bitcast.23, bf16[128,4096]{1,0:T(8,128)(2,1)} %bitcast.21, bf16[128,4096]{1,0:T(8,128)(2,1)} %bitcast.15, bf16[128,4096]{1,0:T(8,128)(2,1)} %bitcast.18, f32[1024,256]{1,0:T(8,128)} %taps_any.3, ...), custom_call_target="tpu_custom_call" | custom-call | flops 524288 | bytes 3145728 | tf_op jit(solution)/shard_map/opening/pallas_call | solution.py:255
  10.9 8.6 %all-to-all-start.1 = ((bf16[16,128,256]{2,1,0:T(8,128)(2,1)}), bf16[16,128,256]{2,1,0:T(8,128)(2,1)S(1)}, u32[]{:S(2)}, u32[]{:S(2)}) async-start(bf16[16,128,256]{2,1,0:T(8,128)(2,1)} %get-tuple-element.34), calls=%async_computation.1 | async-start | bytes 2097152 | tf_op jit(solution)/shard_map/all_to_all | solution.py:675
  19.5 0.0 copy-start.1
  19.5 0.0 copy-start.2
  19.5 0.3 second.1
  19.9 11.6 %all-to-all-done.1 = bf16[16,128,256]{2,1,0:T(8,128)(2,1)S(1)} async-done(((bf16[16,128,256]{2,1,0:T(8,128)(2,1)}), bf16[16,128,256]{2,1,0:T(8,128)(2,1)S(1)}, u32[]{:S(2)}, u32[]{:S(2)}) %all-to-all-start.1) | async-done | bytes 1048608 | tf_op jit(solution)/shard_map/all_to_all | solution.py:675
  31.5 3.7 %all-to-all-start = ((bf16[16,128,256]{2,1,0:T(8,128)(2,1)}), bf16[16,128,256]{2,1,0:T(8,128)(2,1)S(1)}, u32[]{:S(2)}, u32[]{:S(2)}) async-start(bf16[16,128,256]{2,1,0:T(8,128)(2,1)} %get-tuple-element.32), calls=%async_computation | async-start | bytes 2097152 | tf_op jit(solution)/shard_map/all_to_all | solution.py:675
  35.2 0.0 copy-done.4
  35.2 0.0 copy-done.1
  35.2 0.0 copy-done.2
  35.2 10.7 %forward_mix.1 = (bf16[2048,256]{1,0:T(8,128)(2,1)}, bf16[2048,768]{1,0:T(8,128)(2,1)}) custom-call(s32[1,3]{1,0:T(1,128)S(1)} %copy-done.2, bf16[2048,256]{1,0:T(8,128)(2,1)} %bitcast.27, f32[1,256]{1,0:T(1,128)S(1)} %bitcast.13, bf16[2048,1024]{1,0:T(8,128)(2,1)} %constant.4.clone.into_any, bf16[1024,2048]{1,0:T(8,128)(2,1)} %constant.5.clone.back_any, ...), custom_call_target="tpu_custom_call" | custom-call | flops 6442450944 | bytes 25165824 | tf_op jit(solution)/shard_map/forward_mix/pallas_call | solution.py:464
  45.9 2.6 %all-to-all-done = bf16[16,128,256]{2,1,0:T(8,128)(2,1)S(1)} async-done(((bf16[16,128,256]{2,1,0:T(8,128)(2,1)}), bf16[16,128,256]{2,1,0:T(8,128)(2,1)S(1)}, u32[]{:S(2)}, u32[]{:S(2)}) %all-to-all-start) | async-done | bytes 1048608 | tf_op jit(solution)/shard_map/all_to_all | solution.py:675
  48.4 4.1 %all-to-all-start.2 = ((bf16[16,128,256]{2,1,0:T(8,128)(2,1)}), bf16[16,128,256]{2,1,0:T(8,128)(2,1)S(1)}, u32[]{:S(2)}, u32[]{:S(2)}) async-start(bf16[16,128,256]{2,1,0:T(8,128)(2,1)} %bitcast.28), calls=%async_computation.2 | async-start | bytes 2097152 | tf_op jit(solution)/shard_map/all_to_all | solution.py:675
  52.5 0.0 copy-done.3
  52.5 12.6 %backward_mix.1 = (bf16[2048,256]{1,0:T(8,128)(2,1)}, bf16[256,256]{1,0:T(8,128)(2,1)}, bf16[256,256]{1,0:T(8,128)(2,1)}, bf16[256,256]{1,0:T(8,128)(2,1)}, bf16[256,256]{1,0:T(8,128)(2,1)}) custom-call(s32[1,3]{1,0:T(1,128)S(1)} %copy-done.2, bf16[2048,256]{1,0:T(8,128)(2,1)} %bitcast.26, f32[1,256]{1,0:T(1,128)S(1)} %bitcast.14, ...), custom_call_target="tpu_custom_call" | custom-call | flops 7516192768 | bytes 25165824 | tf_op jit(solution)/shard_map/backward_mix/pallas_call | solution.py:584
  65.1 0.0 copy-start
  65.2 1.5 %all-to-all-done.2.inner_any = bf16[16,128,256]{2,1,0:T(8,128)(2,1)S(1)} async-done(((bf16[16,128,256]{2,1,0:T(8,128)(2,1)}), bf16[16,128,256]{2,1,0:T(8,128)(2,1)S(1)}, u32[]{:S(2)}, u32[]{:S(2)}) %all-to-all-start.2) | async-done | bytes 1048608 | tf_op jit(solution)/shard_map/all_to_all | solution.py:675
  66.6 5.3 %all-to-all-start.3 = ((bf16[16,128,256]{2,1,0:T(8,128)(2,1)}), bf16[16,128,256]{2,1,0:T(8,128)(2,1)S(1)}, u32[]{:S(2)}, u32[]{:S(2)}) async-start(bf16[16,128,256]{2,1,0:T(8,128)(2,1)} %bitcast.25), calls=%async_computation.3 | async-start | bytes 2097152 | tf_op jit(solution)/shard_map/all_to_all | solution.py:675
  72.0 1.3 %collective-permute-start = (bf16[256,256]{1,0:T(8,128)(2,1)}, bf16[256,256]{1,0:T(8,128)(2,1)S(1)}, u32[]{:S(2)}, u32[]{:S(2)}) collective-permute-start(bf16[256,256]{1,0:T(8,128)(2,1)} %get-tuple-element.36), channel_id=1, source_target_pairs={{0,32},{16,48},{32,0},{48,16},{64,96},{80,112},{96,64},{112,80},{1... | collective-permute-start | bytes 393224 | tf_op jit(solution)/shard_map/ppermute | solution.py:686
  73.3 2.4 %collective-permute-start.1 = (bf16[256,256]{1,0:T(8,128)(2,1)}, bf16[256,256]{1,0:T(8,128)(2,1)S(1)}, u32[]{:S(2)}, u32[]{:S(2)}) collective-permute-start(bf16[256,256]{1,0:T(8,128)(2,1)} %get-tuple-element.37), channel_id=1, source_target_pairs={{0,64},{16,80},{32,96},{48,112},{64,0},{80,16},{96,32},{112,48},{1... | collective-permute-start | bytes 393224 | tf_op jit(solution)/shard_map/ppermute | solution.py:686
  75.7 0.2 collective-permute-start.2
  75.9 2.6 %gate_both.1 = (bf16[128,4096]{1,0:T(8,128)(2,1)}, bf16[128,4096]{1,0:T(8,128)(2,1)}, bf16[128,4096]{1,0:T(8,128)(2,1)S(1)}) custom-call(bf16[16,128,256]{2,1,0:T(8,128)(2,1)S(1)} %all-to-all-done.2.inner_any, bf16[128,4096]{1,0:T(8,128)(2,1)} %bitcast.20, bf16[128,4096]{1,0:T(8,128)(2,1)} %bitcast.17, bf16[128,4096]{1,0:T(8,128)(2,1)} %bitcast.24), custom_call_target="tpu_custom_call" | custom-call | flops 1048576 | bytes 6291456 | tf_op jit(solution)/shard_map/gate_both/pallas_call | solution.py:122
  78.5 0.0 collective-permute-done.one_ref
  78.5 1.4 %collective-permute-done.1.two_ref = bf16[256,256]{1,0:T(8,128)(2,1)S(1)} collective-permute-done((bf16[256,256]{1,0:T(8,128)(2,1)}, bf16[256,256]{1,0:T(8,128)(2,1)S(1)}, u32[]{:S(2)}, u32[]{:S(2)}) %collective-permute-start.1) | collective-permute-done | bytes 131104 | tf_op jit(solution)/shard_map/ppermute | solution.py:686
  80.0 1.4 %collective-permute-done.2.three_ref = bf16[256,256]{1,0:T(8,128)(2,1)S(1)} collective-permute-done((bf16[256,256]{1,0:T(8,128)(2,1)}, bf16[256,256]{1,0:T(8,128)(2,1)S(1)}, u32[]{:S(2)}, u32[]{:S(2)}) %collective-permute-start.2) | collective-permute-done | bytes 131104 | tf_op jit(solution)/shard_map/ppermute | solution.py:686
  81.4 0.0 copy-done
  81.4 0.1 merge_blocks.1
  81.5 0.1 collective-permute-start.3
  81.6 1.2 %collective-permute-done.3.come_ref = bf16[128,256]{1,0:T(8,128)(2,1)S(1)} collective-permute-done((bf16[128,256]{1,0:T(8,128)(2,1)S(1)}, bf16[128,256]{1,0:T(8,128)(2,1)S(1)}, u32[]{:S(2)}, u32[]{:S(2)}) %collective-permute-start.3) | collective-permute-done | bytes 65568 | tf_op jit(solution)/shard_map/ppermute | solution.py:680
  82.9 0.7 total_blocks.1
  83.5 3.0 %all-to-all-done.3.inner_ref = bf16[16,128,256]{2,1,0:T(8,128)(2,1)S(1)} async-done(((bf16[16,128,256]{2,1,0:T(8,128)(2,1)}), bf16[16,128,256]{2,1,0:T(8,128)(2,1)S(1)}, u32[]{:S(2)}, u32[]{:S(2)}) %all-to-all-start.3) | async-done | bytes 1048608 | tf_op jit(solution)/shard_map/all_to_all | solution.py:675
  86.6 2.4 %gate_last.1 = (bf16[128,4096]{1,0:T(8,128)(2,1)}, bf16[128,4096]{1,0:T(8,128)(2,1)}) custom-call(bf16[16,128,256]{2,1,0:T(8,128)(2,1)S(1)} %all-to-all-done.3.inner_ref, bf16[128,4096]{1,0:T(8,128)(2,1)} %bitcast.22, bf16[128,4096]{1,0:T(8,128)(2,1)S(1)} %get-tuple-element.51.second_ref), custom_call_target="tpu_custom_call" | custom-call | flops 1048576 | bytes 5242880 | tf_op jit(solution)/shard_map/gate_last/pallas_call | solution.py:173
  (2 shorter events, 0.0 us)
Async XLA Ops:
  10.9 20.6 %all-to-all-start.1 = ((bf16[16,128,256]{2,1,0:T(8,128)(2,1)}), bf16[16,128,256]{2,1,0:T(8,128)(2,1)S(1)}, u32[]{:S(2)}, u32[]{:S(2)}) async-start(bf16[16,128,256]{2,1,0:T(8,128)(2,1)} %get-tuple-element.34), calls=%async_computation.1 | async-start | bytes 2097152 | tf_op jit(solution)/shard_map/all_to_all | solution.py:675
  19.5 15.7 %copy-start.1 = (f32[256]{0:T(256)S(1)}, f32[256]{0:T(256)}, u32[]{:S(2)}) copy-start(f32[256]{0:T(256)} %param.14) | copy-start | bytes 3076
  19.5 15.7 %copy-start.2 = (s32[1,3]{1,0:T(1,128)S(1)}, s32[1,3]{1,0:T(1,128)}, u32[]{:S(2)}) copy-start(s32[1,3]{1,0:T(1,128)} %lengths_ref.3) | copy-start | bytes 40
  31.5 3.7 %copy-start.4 = (bf16[16,128,256]{2,1,0:T(8,128)(2,1)}, bf16[16,128,256]{2,1,0:T(8,128)(2,1)S(1)}, u32[]{:S(2)}) copy-start(bf16[16,128,256]{2,1,0:T(8,128)(2,1)S(1)} %all-to-all-done.1) | copy-start | bytes 3145732
  31.5 16.9 %all-to-all-start = ((bf16[16,128,256]{2,1,0:T(8,128)(2,1)}), bf16[16,128,256]{2,1,0:T(8,128)(2,1)S(1)}, u32[]{:S(2)}, u32[]{:S(2)}) async-start(bf16[16,128,256]{2,1,0:T(8,128)(2,1)} %get-tuple-element.32), calls=%async_computation | async-start | bytes 2097152 | tf_op jit(solution)/shard_map/all_to_all | solution.py:675
  48.4 4.1 %copy-start.3 = (bf16[16,128,256]{2,1,0:T(8,128)(2,1)}, bf16[16,128,256]{2,1,0:T(8,128)(2,1)S(1)}, u32[]{:S(2)}) copy-start(bf16[16,128,256]{2,1,0:T(8,128)(2,1)S(1)} %all-to-all-done) | copy-start | bytes 3145732
  48.4 18.2 %all-to-all-start.2 = ((bf16[16,128,256]{2,1,0:T(8,128)(2,1)}), bf16[16,128,256]{2,1,0:T(8,128)(2,1)S(1)}, u32[]{:S(2)}, u32[]{:S(2)}) async-start(bf16[16,128,256]{2,1,0:T(8,128)(2,1)} %bitcast.28), calls=%async_computation.2 | async-start | bytes 2097152 | tf_op jit(solution)/shard_map/all_to_all | solution.py:675
  65.1 16.3 %copy-start = (bf16[256,256]{1,0:T(8,128)(2,1)S(1)}, bf16[256,256]{1,0:T(8,128)(2,1)}, u32[]{:S(2)}) copy-start(bf16[256,256]{1,0:T(8,128)(2,1)} %get-tuple-element.44.own_ref) | copy-start | bytes 393220
  66.6 19.9 %all-to-all-start.3 = ((bf16[16,128,256]{2,1,0:T(8,128)(2,1)}), bf16[16,128,256]{2,1,0:T(8,128)(2,1)S(1)}, u32[]{:S(2)}, u32[]{:S(2)}) async-start(bf16[16,128,256]{2,1,0:T(8,128)(2,1)} %bitcast.25), calls=%async_computation.3 | async-start | bytes 2097152 | tf_op jit(solution)/shard_map/all_to_all | solution.py:675
  72.0 6.5 %collective-permute-start = (bf16[256,256]{1,0:T(8,128)(2,1)}, bf16[256,256]{1,0:T(8,128)(2,1)S(1)}, u32[]{:S(2)}, u32[]{:S(2)}) collective-permute-start(bf16[256,256]{1,0:T(8,128)(2,1)} %get-tuple-element.36), channel_id=1, source_target_pairs={{0,32},{16,48},{32,0},{48,16},{64,96},{80,112},{96,64},{112,80},{1... | collective-permute-start | bytes 393224 | tf_op jit(solution)/shard_map/ppermute | solution.py:686
  73.3 6.7 %collective-permute-start.1 = (bf16[256,256]{1,0:T(8,128)(2,1)}, bf16[256,256]{1,0:T(8,128)(2,1)S(1)}, u32[]{:S(2)}, u32[]{:S(2)}) collective-permute-start(bf16[256,256]{1,0:T(8,128)(2,1)} %get-tuple-element.37), channel_id=1, source_target_pairs={{0,64},{16,80},{32,96},{48,112},{64,0},{80,16},{96,32},{112,48},{1... | collective-permute-start | bytes 393224 | tf_op jit(solution)/shard_map/ppermute | solution.py:686
  75.7 5.7 %collective-permute-start.2 = (bf16[256,256]{1,0:T(8,128)(2,1)}, bf16[256,256]{1,0:T(8,128)(2,1)S(1)}, u32[]{:S(2)}, u32[]{:S(2)}) collective-permute-start(bf16[256,256]{1,0:T(8,128)(2,1)} %get-tuple-element.38), channel_id=1, source_target_pairs={{0,96},{16,112},{32,64},{48,80},{64,32},{80,48},{96,0},{112,16},{1... | collective-permute-start | bytes 393224 | tf_op jit(solution)/shard_map/ppermute | solution.py:686
  81.5 1.3 %collective-permute-start.3 = (bf16[128,256]{1,0:T(8,128)(2,1)S(1)}, bf16[128,256]{1,0:T(8,128)(2,1)S(1)}, u32[]{:S(2)}, u32[]{:S(2)}) collective-permute-start(bf16[128,256]{1,0:T(8,128)(2,1)S(1)} %get-tuple-element.49), channel_id=1, source_target_pairs={{0,16},{16,0},{32,48},{48,32},{64,80},{80,64},{96,112},{112,96},{1... | collective-permute-start | bytes 196616 | tf_op jit(solution)/shard_map/ppermute | solution.py:680

commit v4 on v3

--- a/solution.py
+++ b/solution.py
@@ -182,7 +182,7 @@
     )(near(inner), far(first), near(second))
 
 
-def taps_kernel(taps_any, into_any, out_any, taps_ref, into_ref, out_ref, sems):
+def taps_kernel(meanwhile, taps_any, into_any, out_any, taps_ref, into_ref, out_ref, sems):
     size = out_ref.shape[0]
     tiles = size // TILE
     first = pltpu.make_async_copy(taps_any, taps_ref, sems.at[0, 0])
@@ -193,6 +193,7 @@
         copy = pltpu.make_async_copy(into_any.at[rows], into_ref.at[rows], sems.at[1, tile])
         copy.start()
         loads.append(copy)
+    meanwhile()
     first.wait()
     taps = taps_ref[...].astype(jnp.bfloat16)
     for tile in range(tiles):
@@ -218,8 +219,10 @@
 
     @pl.when(lax.axis_index("dp") % 2 == 1)
     def _():
-        pair_kernel(cot_any, query_any, delta_any, *pair)
-        taps_kernel(taps_any, into_any, spectrum_any, taps_ref, into_ref, spectrum_ref, taps_sems)
+        taps_kernel(
+            lambda: pair_kernel(cot_any, query_any, delta_any, *pair),
+            taps_any, into_any, spectrum_any, taps_ref, into_ref, spectrum_ref, taps_sems,
+        )
 
 
 def second_kernel(
@@ -228,10 +231,11 @@
 ):
     @pl.when(lax.axis_index("dp") % 2 == 0)
     def _():
-        pair_kernel(
-            cot_any, query_any, delta_any, left_ref, right_ref, pair_ref, pair_sems
+        pair = (left_ref, right_ref, pair_ref, pair_sems)
+        taps_kernel(
+            lambda: pair_kernel(cot_any, query_any, delta_any, *pair),
+            taps_any, into_any, spectrum_any, taps_ref, into_ref, spectrum_ref, taps_sems,
         )
-        taps_kernel(taps_any, into_any, spectrum_any, taps_ref, into_ref, spectrum_ref, taps_sems)
 
 
 def opening_scratch(rows, columns, groups, reach, size, width):

time: 89.8 us -> 89.9 us (level)
  waiting for transfers between devices: 22.8 us -> 21.7 us
    all_to_all x4, waiting for transfers between devices: 18.7 us -> 17.7 us  [swap(): lax.all_to_all(pieces, 'ctx', split_axis=0, concat_axis=0, tiled=True)]
where the time goes in v4:
time: 89.9 us; the launch traced here: 89.3 us
  Pallas kernels  40.1 us (45%)
  starting transfers between devices  26.5 us (29%)
  waiting for transfers between devices  21.7 us (24%)
  between operations  0.94 us (1%)
    all_to_all x4, starting transfers between devices, swap(): lax.all_to_all(pieces, 'ctx', split_axis=0, concat_axis=0, tiled=True)  22.5 us
    all_to_all x4, waiting for transfers between devices, swap(): lax.all_to_all(pieces, 'ctx', split_axis=0, concat_axis=0, tiled=True)  17.7 us
    pallas_call x1, Pallas kernels, backward_mix(): pl.pallas_call(backward_kernel, in_specs=[SCALARS, FAR, LOCAL] + [FAR] *...  12.6 us
    pallas_call x1, Pallas kernels, opening(): pl.pallas_call(opening_kernel, in_specs=[FAR] * 6, out_specs=[FAR] * 3, o...  10.7 us
    pallas_call x1, Pallas kernels, forward_mix(): pl.pallas_call(forward_kernel, in_specs=[SCALARS, FAR, LOCAL, FAR, FAR, F...  10.7 us
    ppermute x3, starting transfers between devices, from_chips(): lax.ppermute(block, 'dp', [(i, i ^ 2 * step) for i in range(count)])  3.94 us
    ppermute x3, waiting for transfers between devices, from_chips(): lax.ppermute(block, 'dp', [(i, i ^ 2 * step) for i in range(count)])  2.84 us
    pallas_call x1, Pallas kernels, gate_both(): pl.pallas_call(gate_kernel, in_specs=[pl.BlockSpec(memory_space=pl.ANY)]...  2.6 us
  transfers between devices with their start and end apart: 8, of which 7 were waited for; matrix products, arithmetic and copies ran while one was open for 0% of the time, Pallas kernels for 30%

profile of v4, /device:TPU:1, one launch (start us, length us, event | category | flops | bytes accessed | tf_op | source)
XLA Modules:
  0.0 89.3 jit_solution(10647649215757322791)
XLA Ops:
  0.6 10.7 %opening.1 = (bf16[16,128,256]{2,1,0:T(8,128)(2,1)}, bf16[16,128,256]{2,1,0:T(8,128)(2,1)}, bf16[2048,256]{1,0:T(8,128)(2,1)}) custom-call(bf16[128,4096]{1,0:T(8,128)(2,1)} %bitcast.23, bf16[128,4096]{1,0:T(8,128)(2,1)} %bitcast.21, bf16[128,4096]{1,0:T(8,128)(2,1)} %bitcast.15, bf16[128,4096]{1,0:T(8,128)(2,1)} %bitcast.18, f32[1024,256]{1,0:T(8,128)} %taps_any.3, ...), custom_call_target="tpu_custom_call" | custom-call | flops 524288 | bytes 3145728 | tf_op jit(solution)/shard_map/opening/pallas_call | solution.py:259
  11.3 8.6 %all-to-all-start.1 = ((bf16[16,128,256]{2,1,0:T(8,128)(2,1)}), bf16[16,128,256]{2,1,0:T(8,128)(2,1)S(1)}, u32[]{:S(2)}, u32[]{:S(2)}) async-start(bf16[16,128,256]{2,1,0:T(8,128)(2,1)} %get-tuple-element.34), calls=%async_computation.1 | async-start | bytes 2097152 | tf_op jit(solution)/shard_map/all_to_all | solution.py:679
  19.9 0.0 copy-start.1
  19.9 0.0 copy-start.2
  20.0 0.3 second.1
  20.3 11.8 %all-to-all-done.1 = bf16[16,128,256]{2,1,0:T(8,128)(2,1)S(1)} async-done(((bf16[16,128,256]{2,1,0:T(8,128)(2,1)}), bf16[16,128,256]{2,1,0:T(8,128)(2,1)S(1)}, u32[]{:S(2)}, u32[]{:S(2)}) %all-to-all-start.1) | async-done | bytes 1048608 | tf_op jit(solution)/shard_map/all_to_all | solution.py:679
  32.1 3.7 %all-to-all-start = ((bf16[16,128,256]{2,1,0:T(8,128)(2,1)}), bf16[16,128,256]{2,1,0:T(8,128)(2,1)S(1)}, u32[]{:S(2)}, u32[]{:S(2)}) async-start(bf16[16,128,256]{2,1,0:T(8,128)(2,1)} %get-tuple-element.32), calls=%async_computation | async-start | bytes 2097152 | tf_op jit(solution)/shard_map/all_to_all | solution.py:679
  35.8 0.0 copy-done.4
  35.8 0.0 copy-done.1
  35.8 0.0 copy-done.2
  35.8 10.7 %forward_mix.1 = (bf16[2048,256]{1,0:T(8,128)(2,1)}, bf16[2048,768]{1,0:T(8,128)(2,1)}) custom-call(s32[1,3]{1,0:T(1,128)S(1)} %copy-done.2, bf16[2048,256]{1,0:T(8,128)(2,1)} %bitcast.27, f32[1,256]{1,0:T(1,128)S(1)} %bitcast.13, bf16[2048,1024]{1,0:T(8,128)(2,1)} %constant.4.clone.into_any, bf16[1024,2048]{1,0:T(8,128)(2,1)} %constant.5.clone.back_any, ...), custom_call_target="tpu_custom_call" | custom-call | flops 6442450944 | bytes 25165824 | tf_op jit(solution)/shard_map/forward_mix/pallas_call | solution.py:468
  46.5 2.4 %all-to-all-done = bf16[16,128,256]{2,1,0:T(8,128)(2,1)S(1)} async-done(((bf16[16,128,256]{2,1,0:T(8,128)(2,1)}), bf16[16,128,256]{2,1,0:T(8,128)(2,1)S(1)}, u32[]{:S(2)}, u32[]{:S(2)}) %all-to-all-start) | async-done | bytes 1048608 | tf_op jit(solution)/shard_map/all_to_all | solution.py:679
  48.8 4.3 %all-to-all-start.2 = ((bf16[16,128,256]{2,1,0:T(8,128)(2,1)}), bf16[16,128,256]{2,1,0:T(8,128)(2,1)S(1)}, u32[]{:S(2)}, u32[]{:S(2)}) async-start(bf16[16,128,256]{2,1,0:T(8,128)(2,1)} %bitcast.28), calls=%async_computation.2 | async-start | bytes 2097152 | tf_op jit(solution)/shard_map/all_to_all | solution.py:679
  53.1 0.0 copy-done.3
  53.1 12.6 %backward_mix.1 = (bf16[2048,256]{1,0:T(8,128)(2,1)}, bf16[256,256]{1,0:T(8,128)(2,1)}, bf16[256,256]{1,0:T(8,128)(2,1)}, bf16[256,256]{1,0:T(8,128)(2,1)}, bf16[256,256]{1,0:T(8,128)(2,1)}) custom-call(s32[1,3]{1,0:T(1,128)S(1)} %copy-done.2, bf16[2048,256]{1,0:T(8,128)(2,1)} %bitcast.26, f32[1,256]{1,0:T(1,128)S(1)} %bitcast.14, ...), custom_call_target="tpu_custom_call" | custom-call | flops 7516192768 | bytes 25165824 | tf_op jit(solution)/shard_map/backward_mix/pallas_call | solution.py:588
  65.8 0.0 copy-start
  65.8 0.9 all-to-all-done.2.inner_any
  66.7 5.9 %all-to-all-start.3 = ((bf16[16,128,256]{2,1,0:T(8,128)(2,1)}), bf16[16,128,256]{2,1,0:T(8,128)(2,1)S(1)}, u32[]{:S(2)}, u32[]{:S(2)}) async-start(bf16[16,128,256]{2,1,0:T(8,128)(2,1)} %bitcast.25), calls=%async_computation.3 | async-start | bytes 2097152 | tf_op jit(solution)/shard_map/all_to_all | solution.py:679
  72.6 1.3 %collective-permute-start = (bf16[256,256]{1,0:T(8,128)(2,1)}, bf16[256,256]{1,0:T(8,128)(2,1)S(1)}, u32[]{:S(2)}, u32[]{:S(2)}) collective-permute-start(bf16[256,256]{1,0:T(8,128)(2,1)} %get-tuple-element.36), channel_id=1, source_target_pairs={{0,32},{16,48},{32,0},{48,16},{64,96},{80,112},{96,64},{112,80},{1... | collective-permute-start | bytes 393224 | tf_op jit(solution)/shard_map/ppermute | solution.py:690
  73.9 2.5 %collective-permute-start.1 = (bf16[256,256]{1,0:T(8,128)(2,1)}, bf16[256,256]{1,0:T(8,128)(2,1)S(1)}, u32[]{:S(2)}, u32[]{:S(2)}) collective-permute-start(bf16[256,256]{1,0:T(8,128)(2,1)} %get-tuple-element.37), channel_id=1, source_target_pairs={{0,64},{16,80},{32,96},{48,112},{64,0},{80,16},{96,32},{112,48},{1... | collective-permute-start | bytes 393224 | tf_op jit(solution)/shard_map/ppermute | solution.py:690
  76.3 0.2 collective-permute-start.2
  76.5 2.6 %gate_both.1 = (bf16[128,4096]{1,0:T(8,128)(2,1)}, bf16[128,4096]{1,0:T(8,128)(2,1)}, bf16[128,4096]{1,0:T(8,128)(2,1)S(1)}) custom-call(bf16[16,128,256]{2,1,0:T(8,128)(2,1)S(1)} %all-to-all-done.2.inner_any, bf16[128,4096]{1,0:T(8,128)(2,1)} %bitcast.20, bf16[128,4096]{1,0:T(8,128)(2,1)} %bitcast.17, bf16[128,4096]{1,0:T(8,128)(2,1)} %bitcast.24), custom_call_target="tpu_custom_call" | custom-call | flops 1048576 | bytes 6291456 | tf_op jit(solution)/shard_map/gate_both/pallas_call | solution.py:122
  79.1 0.0 collective-permute-done.one_ref
  79.1 1.1 %collective-permute-done.1.two_ref = bf16[256,256]{1,0:T(8,128)(2,1)S(1)} collective-permute-done((bf16[256,256]{1,0:T(8,128)(2,1)}, bf16[256,256]{1,0:T(8,128)(2,1)S(1)}, u32[]{:S(2)}, u32[]{:S(2)}) %collective-permute-start.1) | collective-permute-done | bytes 131104 | tf_op jit(solution)/shard_map/ppermute | solution.py:690
  80.3 1.7 %collective-permute-done.2.three_ref = bf16[256,256]{1,0:T(8,128)(2,1)S(1)} collective-permute-done((bf16[256,256]{1,0:T(8,128)(2,1)}, bf16[256,256]{1,0:T(8,128)(2,1)S(1)}, u32[]{:S(2)}, u32[]{:S(2)}) %collective-permute-start.2) | collective-permute-done | bytes 131104 | tf_op jit(solution)/shard_map/ppermute | solution.py:690
  82.0 0.0 copy-done
  82.0 0.1 merge_blocks.1
  82.1 0.1 collective-permute-start.3
  82.2 1.2 %collective-permute-done.3.come_ref = bf16[128,256]{1,0:T(8,128)(2,1)S(1)} collective-permute-done((bf16[128,256]{1,0:T(8,128)(2,1)S(1)}, bf16[128,256]{1,0:T(8,128)(2,1)S(1)}, u32[]{:S(2)}, u32[]{:S(2)}) %collective-permute-start.3) | collective-permute-done | bytes 65568 | tf_op jit(solution)/shard_map/ppermute | solution.py:684
  83.5 0.7 total_blocks.1
  84.1 2.6 %all-to-all-done.3.inner_ref = bf16[16,128,256]{2,1,0:T(8,128)(2,1)S(1)} async-done(((bf16[16,128,256]{2,1,0:T(8,128)(2,1)}), bf16[16,128,256]{2,1,0:T(8,128)(2,1)S(1)}, u32[]{:S(2)}, u32[]{:S(2)}) %all-to-all-start.3) | async-done | bytes 1048608 | tf_op jit(solution)/shard_map/all_to_all | solution.py:679
  86.7 2.4 %gate_last.1 = (bf16[128,4096]{1,0:T(8,128)(2,1)}, bf16[128,4096]{1,0:T(8,128)(2,1)}) custom-call(bf16[16,128,256]{2,1,0:T(8,128)(2,1)S(1)} %all-to-all-done.3.inner_ref, bf16[128,4096]{1,0:T(8,128)(2,1)} %bitcast.22, bf16[128,4096]{1,0:T(8,128)(2,1)S(1)} %get-tuple-element.51.second_ref), custom_call_target="tpu_custom_call" | custom-call | flops 1048576 | bytes 5242880 | tf_op jit(solution)/shard_map/gate_last/pallas_call | solution.py:173
  (2 shorter events, 0.0 us)
Async XLA Ops:
  11.3 20.8 %all-to-all-start.1 = ((bf16[16,128,256]{2,1,0:T(8,128)(2,1)}), bf16[16,128,256]{2,1,0:T(8,128)(2,1)S(1)}, u32[]{:S(2)}, u32[]{:S(2)}) async-start(bf16[16,128,256]{2,1,0:T(8,128)(2,1)} %get-tuple-element.34), calls=%async_computation.1 | async-start | bytes 2097152 | tf_op jit(solution)/shard_map/all_to_all | solution.py:679
  19.9 15.9 %copy-start.1 = (f32[256]{0:T(256)S(1)}, f32[256]{0:T(256)}, u32[]{:S(2)}) copy-start(f32[256]{0:T(256)} %param.14) | copy-start | bytes 3076
  19.9 15.9 %copy-start.2 = (s32[1,3]{1,0:T(1,128)S(1)}, s32[1,3]{1,0:T(1,128)}, u32[]{:S(2)}) copy-start(s32[1,3]{1,0:T(1,128)} %lengths_ref.3) | copy-start | bytes 40
  32.1 3.7 %copy-start.4 = (bf16[16,128,256]{2,1,0:T(8,128)(2,1)}, bf16[16,128,256]{2,1,0:T(8,128)(2,1)S(1)}, u32[]{:S(2)}) copy-start(bf16[16,128,256]{2,1,0:T(8,128)(2,1)S(1)} %all-to-all-done.1) | copy-start | bytes 3145732
  32.1 16.7 %all-to-all-start = ((bf16[16,128,256]{2,1,0:T(8,128)(2,1)}), bf16[16,128,256]{2,1,0:T(8,128)(2,1)S(1)}, u32[]{:S(2)}, u32[]{:S(2)}) async-start(bf16[16,128,256]{2,1,0:T(8,128)(2,1)} %get-tuple-element.32), calls=%async_computation | async-start | bytes 2097152 | tf_op jit(solution)/shard_map/all_to_all | solution.py:679
  48.8 4.3 %copy-start.3 = (bf16[16,128,256]{2,1,0:T(8,128)(2,1)}, bf16[16,128,256]{2,1,0:T(8,128)(2,1)S(1)}, u32[]{:S(2)}) copy-start(bf16[16,128,256]{2,1,0:T(8,128)(2,1)S(1)} %all-to-all-done) | copy-start | bytes 3145732
  48.8 17.8 %all-to-all-start.2 = ((bf16[16,128,256]{2,1,0:T(8,128)(2,1)}), bf16[16,128,256]{2,1,0:T(8,128)(2,1)S(1)}, u32[]{:S(2)}, u32[]{:S(2)}) async-start(bf16[16,128,256]{2,1,0:T(8,128)(2,1)} %bitcast.28), calls=%async_computation.2 | async-start | bytes 2097152 | tf_op jit(solution)/shard_map/all_to_all | solution.py:679
  65.8 16.2 %copy-start = (bf16[256,256]{1,0:T(8,128)(2,1)S(1)}, bf16[256,256]{1,0:T(8,128)(2,1)}, u32[]{:S(2)}) copy-start(bf16[256,256]{1,0:T(8,128)(2,1)} %get-tuple-element.44.own_ref) | copy-start | bytes 393220
  66.7 20.1 %all-to-all-start.3 = ((bf16[16,128,256]{2,1,0:T(8,128)(2,1)}), bf16[16,128,256]{2,1,0:T(8,128)(2,1)S(1)}, u32[]{:S(2)}, u32[]{:S(2)}) async-start(bf16[16,128,256]{2,1,0:T(8,128)(2,1)} %bitcast.25), calls=%async_computation.3 | async-start | bytes 2097152 | tf_op jit(solution)/shard_map/all_to_all | solution.py:679
  72.6 6.5 %collective-permute-start = (bf16[256,256]{1,0:T(8,128)(2,1)}, bf16[256,256]{1,0:T(8,128)(2,1)S(1)}, u32[]{:S(2)}, u32[]{:S(2)}) collective-permute-start(bf16[256,256]{1,0:T(8,128)(2,1)} %get-tuple-element.36), channel_id=1, source_target_pairs={{0,32},{16,48},{32,0},{48,16},{64,96},{80,112},{96,64},{112,80},{1... | collective-permute-start | bytes 393224 | tf_op jit(solution)/shard_map/ppermute | solution.py:690
  73.9 6.4 %collective-permute-start.1 = (bf16[256,256]{1,0:T(8,128)(2,1)}, bf16[256,256]{1,0:T(8,128)(2,1)S(1)}, u32[]{:S(2)}, u32[]{:S(2)}) collective-permute-start(bf16[256,256]{1,0:T(8,128)(2,1)} %get-tuple-element.37), channel_id=1, source_target_pairs={{0,64},{16,80},{32,96},{48,112},{64,0},{80,16},{96,32},{112,48},{1... | collective-permute-start | bytes 393224 | tf_op jit(solution)/shard_map/ppermute | solution.py:690
  76.3 5.7 %collective-permute-start.2 = (bf16[256,256]{1,0:T(8,128)(2,1)}, bf16[256,256]{1,0:T(8,128)(2,1)S(1)}, u32[]{:S(2)}, u32[]{:S(2)}) collective-permute-start(bf16[256,256]{1,0:T(8,128)(2,1)} %get-tuple-element.38), channel_id=1, source_target_pairs={{0,96},{16,112},{32,64},{48,80},{64,32},{80,48},{96,0},{112,16},{1... | collective-permute-start | bytes 393224 | tf_op jit(solution)/shard_map/ppermute | solution.py:690
  82.1 1.3 %collective-permute-start.3 = (bf16[128,256]{1,0:T(8,128)(2,1)S(1)}, bf16[128,256]{1,0:T(8,128)(2,1)S(1)}, u32[]{:S(2)}, u32[]{:S(2)}) collective-permute-start(bf16[128,256]{1,0:T(8,128)(2,1)S(1)} %get-tuple-element.49), channel_id=1, source_target_pairs={{0,16},{16,0},{32,48},{48,32},{64,80},{80,64},{96,112},{112,96},{1... | collective-permute-start | bytes 196616 | tf_op jit(solution)/shard_map/ppermute | solution.py:684
